TPU v7x, 32 devices: a whole 2x2x4 slice. The times are simulated.
32 devices in a mesh: dp: 8 (over y, x, core), seq: 4 (over z).
Axes of the slice: x: 2, y: 2, z: 4, core: 2. Of those that a mesh axis runs over, the one named last changes fastest.
Arguments:
- latents: bfloat16 [2, 16, 256, 768], P(None, 'dp', 'seq'), may hold values from -6 to 6
- conditions: bfloat16 [2, 16, 768], P(None, 'dp'), may hold values from -6 to 6
- modulator: bfloat16 [768, 4608], P('dp', 'seq'), may hold values from -0.21875 to 0.21875
- modbias: bfloat16 [4608], P('seq'), may hold values from -3 to 3
- qkvweight: bfloat16 [768, 2304], P('dp', 'seq'), may hold values from -0.21875 to 0.21875
- querybias: bfloat16 [768], P('seq'), may hold values from -3 to 3
- valuebias: bfloat16 [768], P('seq'), may hold values from -3 to 3
- projection: bfloat16 [768, 768], P('dp', 'seq'), may hold values from -0.875 to 0.875
- projbias: bfloat16 [768], P('seq'), may hold values from -3 to 3
- expand: bfloat16 [768, 3072], P('dp', 'seq'), may hold values from -0.21875 to 0.21875
- expandbias: bfloat16 [3072], P('seq'), may hold values from -3 to 3
- contract: bfloat16 [3072, 768], P('dp', 'seq'), may hold values from -0.109375 to 0.109375
- contractbias: bfloat16 [768], P('seq'), may hold values from -3 to 3
- cotangent: bfloat16 [2, 16, 256, 768], P(None, 'dp', 'seq'), may hold values from -6 to 6
Outputs:
- result: bfloat16 [2, 16, 256, 768], P(None, 'dp', 'seq')
- latents_grad: bfloat16 [2, 16, 256, 768], P(None, 'dp', 'seq')
- conditions_grad: float32 [2, 16, 768], P(None, 'dp')
- modulator_grad: float32 [768, 4608], P('dp', 'seq')
- modbias_grad: float32 [4608], P('seq')
- qkvweight_grad: float32 [768, 2304], P('dp', 'seq')
- querybias_grad: float32 [768], P('seq')
- valuebias_grad: float32 [768], P('seq')
- projection_grad: float32 [768, 768], P('dp', 'seq')
- projbias_grad: float32 [768], P('seq')
- expand_grad: float32 [768, 3072], P('dp', 'seq')
- expandbias_grad: float32 [3072], P('seq')
- contract_grad: float32 [3072, 768], P('dp', 'seq')
- contractbias_grad: float32 [768], P('seq')
All inputs are finite; a program needn't handle non-finite values.
Results may differ from a plain program's by a relative error of at most 0.04.
Values may be sent and summed in bfloat16 or wider, within the bound.
No kernel may reach another device: no remote copies, remote signals or barrier semaphores. Data moves between devices by JAX's collectives and lax.ppermute only.
A program may use at most 128 MiB of HBM per device.

v0:
```python
import jax
import jax.numpy as jnp
from jax import lax
from jax.sharding import PartitionSpec as P

H = 12


EPSILON = 1e-06


def normalize(values):
    center = values - jnp.mean(values, axis=-1, keepdims=True)
    inverse = lax.rsqrt(jnp.mean(center * center, axis=-1, keepdims=True) + EPSILON)
    return (center * inverse, inverse)


def norm_back(grad_normed, normed, inverse):
    first = jnp.mean(grad_normed, axis=-1, keepdims=True)
    second = jnp.mean(grad_normed * normed, axis=-1, keepdims=True)
    return inverse * (grad_normed - first - normed * second)


def project(values, matrix):
    return jnp.einsum("lsd,dn->lsn", values, matrix, preferred_element_type=jnp.float32)


def project_back(grads, matrix):
    return jnp.einsum("lsn,dn->lsd", grads, matrix, preferred_element_type=jnp.float32)


def outer_sum(values, grads):
    return jnp.einsum("lsd,lsn->dn", values, grads, preferred_element_type=jnp.float32)


def column_sum(grads):
    return jnp.sum(grads.astype(jnp.float32), axis=(0, 1))


def gelu_tanh(values):
    return jax.nn.gelu(values, approximate=True)


def assemble(full):
    return (
        full[0],
        full[5],
        full[1],
        full[6],
        full[7],
        full[2],
        full[8],
        full[3],
        full[9],
        full[4],
        full[10],
    )


def forward_micro(weights, tokens_low, conds_low):
    (
        mod_matrix,
        mod_offset,
        qkv_matrix,
        query_offset,
        value_offset,
        proj_matrix,
        proj_offset,
        up_matrix,
        up_offset,
        down_matrix,
        down_offset,
    ) = weights
    lat_count, length, width = tokens_low.shape
    head_size = width // H
    factor = head_size ** (-0.5)
    cond_float = conds_low.astype(jnp.float32)
    cond_act = jax.nn.silu(cond_float).astype(jnp.bfloat16)
    modulation = jnp.dot(
        cond_act, mod_matrix, preferred_element_type=jnp.float32
    ) + mod_offset.astype(jnp.float32)
    pieces = jnp.split(modulation[:, None, :], 6, axis=-1)
    tokens = tokens_low.astype(jnp.float32)
    normed1, inverse1 = normalize(tokens)
    hidden1 = (normed1 * (1.0 + pieces[1]) + pieces[0]).astype(jnp.bfloat16)
    offsets = jnp.concatenate([query_offset, jnp.zeros_like(query_offset), value_offset]).astype(
        jnp.float32
    )
    qkv_low = (project(hidden1, qkv_matrix) + offsets).astype(jnp.bfloat16)
    queries = qkv_low[..., :width].reshape(lat_count, length, H, head_size)
    keys = qkv_low[..., width : 2 * width].reshape(lat_count, length, H, head_size)
    values = qkv_low[..., 2 * width :].reshape(lat_count, length, H, head_size)
    all_keys, all_values = (
        lax.all_gather(keys, "seq", axis=1, tiled=True),
        lax.all_gather(values, "seq", axis=1, tiled=True),
    )
    scores = (
        jnp.einsum("lshd,lthd->lhst", queries, all_keys, preferred_element_type=jnp.float32)
        * factor
    )
    highest = jnp.max(scores, axis=-1, keepdims=True)
    expo = jnp.exp(scores - highest)
    totals = jnp.sum(expo, axis=-1, keepdims=True)
    probs_low = (expo / totals).astype(jnp.bfloat16)
    logsum = highest + jnp.log(totals)
    attended = jnp.einsum(
        "lhst,lthd->lshd", probs_low, all_values, preferred_element_type=jnp.float32
    )
    attended = attended.reshape(lat_count, length, width).astype(jnp.bfloat16)
    branch1 = project(attended, proj_matrix) + proj_offset.astype(jnp.float32)
    middle = tokens + pieces[2] * branch1
    normed2, inverse2 = normalize(middle)
    hidden2 = (normed2 * (1.0 + pieces[4]) + pieces[3]).astype(jnp.bfloat16)
    before = project(hidden2, up_matrix) + up_offset.astype(jnp.float32)
    active = gelu_tanh(before).astype(jnp.bfloat16)
    branch2 = project(active, down_matrix) + down_offset.astype(jnp.float32)
    output = (middle + pieces[5] * branch2).astype(jnp.bfloat16)
    kept = (
        cond_float,
        cond_act,
        pieces,
        normed1,
        inverse1,
        hidden1,
        queries,
        all_keys,
        all_values,
        logsum,
        attended,
        branch1,
        normed2,
        inverse2,
        hidden2,
        before,
        active,
        branch2,
    )
    return (output, kept)


def backward_micro(weights, kept, cot_low, owner_mask):
    (
        mod_matrix,
        mod_offset,
        qkv_matrix,
        query_offset,
        value_offset,
        proj_matrix,
        proj_offset,
        up_matrix,
        up_offset,
        down_matrix,
        down_offset,
    ) = weights
    (
        cond_float,
        cond_act,
        pieces,
        normed1,
        inverse1,
        hidden1,
        queries,
        all_keys,
        all_values,
        logsum,
        attended,
        branch1,
        normed2,
        inverse2,
        hidden2,
        before,
        active,
        branch2,
    ) = kept
    lat_count, length, heads, head_size = queries.shape
    width = heads * head_size
    factor = head_size ** (-0.5)
    dout = cot_low.astype(jnp.float32)
    dbranch2 = (pieces[5] * dout).astype(jnp.bfloat16)
    dgate2 = jnp.sum(dout * branch2, axis=1)
    grad_down = outer_sum(active, dbranch2)
    grad_down_offset = column_sum(dbranch2)
    dactive = project_back(dbranch2, down_matrix)
    dbefore = jax.vjp(gelu_tanh, before)[1](dactive)[0].astype(jnp.bfloat16)
    grad_up = outer_sum(hidden2, dbefore)
    grad_up_offset = column_sum(dbefore)
    dhidden2 = project_back(dbefore, up_matrix)
    dshift2 = jnp.sum(dhidden2, axis=1)
    dscale2 = jnp.sum(dhidden2 * normed2, axis=1)
    dmiddle = dout + norm_back(dhidden2 * (1.0 + pieces[4]), normed2, inverse2)
    dbranch1 = (pieces[2] * dmiddle).astype(jnp.bfloat16)
    dgate1 = jnp.sum(dmiddle * branch1, axis=1)
    grad_proj = outer_sum(attended, dbranch1)
    grad_proj_offset = column_sum(dbranch1)
    dattended = project_back(dbranch1, proj_matrix).astype(jnp.bfloat16)
    dattended = dattended.reshape(lat_count, length, heads, head_size)
    scores = (
        jnp.einsum("lshd,lthd->lhst", queries, all_keys, preferred_element_type=jnp.float32)
        * factor
    )
    probs = jnp.exp(scores - logsum)
    dprobs = jnp.einsum(
        "lshd,lthd->lhst", dattended, all_values, preferred_element_type=jnp.float32
    )
    rowsum = jnp.sum(dprobs * probs, axis=-1, keepdims=True)
    dscores = (probs * (dprobs - rowsum)).astype(jnp.bfloat16)
    dqueries = (
        jnp.einsum("lhst,lthd->lshd", dscores, all_keys, preferred_element_type=jnp.float32)
        * factor
    )
    dkeys_part = (
        jnp.einsum("lhst,lshd->lthd", dscores, queries, preferred_element_type=jnp.float32) * factor
    )
    dvalues_part = jnp.einsum(
        "lhst,lshd->lthd", probs.astype(jnp.bfloat16), dattended, preferred_element_type=jnp.float32
    )
    dkeys, dvalues = (
        lax.psum_scatter(
            dkeys_part.astype(jnp.bfloat16), "seq", scatter_dimension=1, tiled=True
        ).astype(jnp.float32),
        lax.psum_scatter(
            dvalues_part.astype(jnp.bfloat16), "seq", scatter_dimension=1, tiled=True
        ).astype(jnp.float32),
    )
    dqkv = jnp.concatenate(
        [
            dqueries.reshape(lat_count, length, width),
            dkeys.reshape(lat_count, length, width),
            dvalues.reshape(lat_count, length, width),
        ],
        axis=-1,
    ).astype(jnp.bfloat16)
    grad_qkv = outer_sum(hidden1, dqkv)
    grad_query_offset = column_sum(dqkv[..., :width])
    grad_value_offset = column_sum(dqkv[..., 2 * width :])
    dhidden1 = project_back(dqkv, qkv_matrix)
    dshift1 = jnp.sum(dhidden1, axis=1)
    dscale1 = jnp.sum(dhidden1 * normed1, axis=1)
    dtokens = dmiddle + norm_back(dhidden1 * (1.0 + pieces[1]), normed1, inverse1)
    dmod_part = jnp.concatenate([dshift1, dscale1, dgate1, dshift2, dscale2, dgate2], axis=-1)
    dmod = lax.psum(dmod_part.astype(jnp.bfloat16), "seq")
    dmod_owned = jnp.where(owner_mask[:, None], dmod, jnp.zeros_like(dmod))
    grad_mod = jnp.einsum("ld,ln->dn", cond_act, dmod_owned, preferred_element_type=jnp.float32)
    grad_mod_offset = jnp.sum(dmod_owned.astype(jnp.float32), axis=0)
    dcond_act = jnp.einsum("ln,dn->ld", dmod, mod_matrix, preferred_element_type=jnp.float32)
    dconds = jax.vjp(jax.nn.silu, cond_float)[1](dcond_act)[0]
    grads = (
        grad_mod,
        grad_mod_offset,
        grad_qkv,
        grad_query_offset,
        grad_value_offset,
        grad_proj,
        grad_proj_offset,
        grad_up,
        grad_up_offset,
        grad_down,
        grad_down_offset,
    )
    return (dtokens.astype(jnp.bfloat16), dconds, grads)


def local(
    latents,
    conditions,
    modulator,
    modbias,
    qkvweight,
    querybias,
    valuebias,
    projection,
    projbias,
    expand,
    expandbias,
    contract,
    contractbias,
    cotangent,
):
    rows = (
        lax.all_gather(modulator, "dp", axis=0, tiled=True),
        lax.all_gather(qkvweight, "dp", axis=0, tiled=True),
        lax.all_gather(projection, "dp", axis=0, tiled=True),
        lax.all_gather(expand, "dp", axis=0, tiled=True),
        lax.all_gather(contract, "dp", axis=0, tiled=True),
    )
    full = (
        lax.all_gather(rows[0], "seq", axis=1, tiled=True),
        lax.all_gather(rows[1], "seq", axis=1, tiled=True),
        lax.all_gather(rows[2], "seq", axis=1, tiled=True),
        lax.all_gather(rows[3], "seq", axis=1, tiled=True),
        lax.all_gather(rows[4], "seq", axis=1, tiled=True),
        lax.all_gather(modbias, "seq", axis=0, tiled=True),
        lax.all_gather(querybias, "seq", axis=0, tiled=True),
        lax.all_gather(valuebias, "seq", axis=0, tiled=True),
        lax.all_gather(projbias, "seq", axis=0, tiled=True),
        lax.all_gather(expandbias, "seq", axis=0, tiled=True),
        lax.all_gather(contractbias, "seq", axis=0, tiled=True),
    )
    weights = assemble(full)
    batch_count = latents.shape[0]
    lat_count = latents.shape[1]
    outputs = []
    stored = []
    for batch_index in range(batch_count):
        output, kept = forward_micro(weights, latents[batch_index], conditions[batch_index])
        outputs.append(output)
        stored.append(kept)
    rows_back = (
        lax.all_gather(modulator, "dp", axis=0, tiled=True),
        lax.all_gather(qkvweight, "dp", axis=0, tiled=True),
        lax.all_gather(projection, "dp", axis=0, tiled=True),
        lax.all_gather(expand, "dp", axis=0, tiled=True),
        lax.all_gather(contract, "dp", axis=0, tiled=True),
    )
    full_back = (
        lax.all_gather(rows_back[0], "seq", axis=1, tiled=True),
        lax.all_gather(rows_back[1], "seq", axis=1, tiled=True),
        lax.all_gather(rows_back[2], "seq", axis=1, tiled=True),
        lax.all_gather(rows_back[3], "seq", axis=1, tiled=True),
        lax.all_gather(rows_back[4], "seq", axis=1, tiled=True),
        lax.all_gather(modbias, "seq", axis=0, tiled=True),
        lax.all_gather(querybias, "seq", axis=0, tiled=True),
        lax.all_gather(valuebias, "seq", axis=0, tiled=True),
        lax.all_gather(projbias, "seq", axis=0, tiled=True),
        lax.all_gather(expandbias, "seq", axis=0, tiled=True),
        lax.all_gather(contractbias, "seq", axis=0, tiled=True),
    )
    back_weights = assemble(full_back)
    owner_mask = jnp.arange(lat_count) % lax.axis_size("seq") == lax.axis_index("seq")
    accumulated = tuple((jnp.zeros(w.shape, jnp.float32) for w in back_weights))
    token_grads = []
    cond_grads = []
    for batch_index in range(batch_count):
        dtokens, dconds, grads = backward_micro(
            back_weights, stored[batch_index], cotangent[batch_index], owner_mask
        )
        token_grads.append(dtokens)
        cond_grads.append(dconds)
        accumulated = tuple((a + b for a, b in zip(accumulated, grads)))
    columns = (
        lax.psum_scatter(
            accumulated[0].astype(jnp.bfloat16), "seq", scatter_dimension=1, tiled=True
        ).astype(jnp.float32),
        lax.psum_scatter(
            accumulated[2].astype(jnp.bfloat16), "seq", scatter_dimension=1, tiled=True
        ).astype(jnp.float32),
        lax.psum_scatter(
            accumulated[5].astype(jnp.bfloat16), "seq", scatter_dimension=1, tiled=True
        ).astype(jnp.float32),
        lax.psum_scatter(
            accumulated[7].astype(jnp.bfloat16), "seq", scatter_dimension=1, tiled=True
        ).astype(jnp.float32),
        lax.psum_scatter(
            accumulated[9].astype(jnp.bfloat16), "seq", scatter_dimension=1, tiled=True
        ).astype(jnp.float32),
        lax.psum_scatter(
            accumulated[1].astype(jnp.bfloat16), "seq", scatter_dimension=0, tiled=True
        ).astype(jnp.float32),
        lax.psum_scatter(
            accumulated[3].astype(jnp.bfloat16), "seq", scatter_dimension=0, tiled=True
        ).astype(jnp.float32),
        lax.psum_scatter(
            accumulated[4].astype(jnp.bfloat16), "seq", scatter_dimension=0, tiled=True
        ).astype(jnp.float32),
        lax.psum_scatter(
            accumulated[6].astype(jnp.bfloat16), "seq", scatter_dimension=0, tiled=True
        ).astype(jnp.float32),
        lax.psum_scatter(
            accumulated[8].astype(jnp.bfloat16), "seq", scatter_dimension=0, tiled=True
        ).astype(jnp.float32),
        lax.psum_scatter(
            accumulated[10].astype(jnp.bfloat16), "seq", scatter_dimension=0, tiled=True
        ).astype(jnp.float32),
    )
    owned_rows = (
        lax.psum_scatter(columns[0], "dp", scatter_dimension=0, tiled=True),
        lax.psum_scatter(columns[1], "dp", scatter_dimension=0, tiled=True),
        lax.psum_scatter(columns[2], "dp", scatter_dimension=0, tiled=True),
        lax.psum_scatter(columns[3], "dp", scatter_dimension=0, tiled=True),
        lax.psum_scatter(columns[4], "dp", scatter_dimension=0, tiled=True),
    )
    owned_offsets = lax.psum(
        (columns[5], columns[6], columns[7], columns[8], columns[9], columns[10]), "dp"
    )
    return (
        jnp.stack(outputs),
        jnp.stack(token_grads),
        jnp.stack(cond_grads),
        owned_rows[0],
        owned_offsets[0],
        owned_rows[1],
        owned_offsets[1],
        owned_offsets[2],
        owned_rows[2],
        owned_offsets[3],
        owned_rows[3],
        owned_offsets[4],
        owned_rows[4],
        owned_offsets[5],
    )


def solution(mesh):
    placed = (
        P(None, "dp", "seq", None),
        P(None, "dp", None),
        P("dp", "seq"),
        P("seq"),
        P("dp", "seq"),
        P("seq"),
        P("seq"),
        P("dp", "seq"),
        P("seq"),
        P("dp", "seq"),
        P("seq"),
        P("dp", "seq"),
        P("seq"),
        P(None, "dp", "seq", None),
    )
    return jax.shard_map(
        local,
        mesh=mesh,
        in_specs=placed,
        out_specs=(
            P(None, "dp", "seq", None),
            P(None, "dp", "seq", None),
            P(None, "dp", None),
            P("dp", "seq"),
            P("seq"),
            P("dp", "seq"),
            P("seq"),
            P("seq"),
            P("dp", "seq"),
            P("seq"),
            P("dp", "seq"),
            P("seq"),
            P("dp", "seq"),
            P("seq"),
        ),
        check_vma=False,
    )
```

profile of v0, /device:TPU:0, one launch (start us, length us, event | category | flops | bytes accessed | tf_op | source)
XLA Modules:
  0.0 1337.3 jit_solution(16143328648510298443)
XLA Ops:
  9.5 29.7 %all-gather.11.cloned.1.call-done = bf16[768,1152]{1,0:T(8,128)(2,1)} async-done(((bf16[96,1152]{1,0:T(8,128)(2,1)}), bf16[768,1152]{1,0:T(8,128)(2,1)}) %all-gather.11.cloned.1.call-update) | async-done | bytes 1769488 | tf_op jit(solution)/shard_map/all_gather | solution.py:280
  39.2 10.8 all_gather.73
  51.4 8.8 all_gather.79
  61.1 4.0 all-gather.19.cloned.1.call-done
  67.5 11.8 all-reduce.13
  79.9 13.0 all-gather.1
  93.0 13.1 all-gather
  106.8 114.1 %all-gather.13.cloned.1.call-done = bf16[768,4608]{1,0:T(8,128)(2,1)} async-done(((bf16[768,1152]{1,0:T(8,128)(2,1)}), bf16[768,4608]{1,0:T(8,128)(2,1)}) %all-gather.13.cloned.1.call-update) | async-done | bytes 7077904 | tf_op jit(solution)/shard_map/all_gather | solution.py:287
  220.9 4.0 fusion.4
  225.0 65.5 %all-gather.15.cloned.1.call-done = bf16[768,2304]{0,1:T(8,128)(2,1)} async-done(((bf16[768,576]{0,1:T(8,128)(2,1)}), bf16[768,2304]{0,1:T(8,128)(2,1)}) %all-gather.15.cloned.1.call-update) | async-done | bytes 3538960 | tf_op jit(solution)/shard_map/all_gather | solution.py:288
  290.5 3.3 fusion.28
  295.3 4.3 fusion.3
  303.6 43.2 %all_gather.89 = bf16[2,256,12,64]{3,1,2,0:T(8,128)(2,1)S(1)} all-gather(bf16[2,64,12,64]{3,1,2,0:T(8,128)(2,1)S(1)} %copy.160), channel_id=1, replica_groups=mesh['dp'=8,'seq'=4] {'seq'}, dimensions={1}, use_global_device_ids=true | all-gather | bytes 983040 | tf_op jit(solution)/shard_map/all_gather | solution.py:94
  348.6 54.6 %all_gather.78 = bf16[2,256,12,64]{3,1,2,0:T(8,128)(2,1)S(1)} all-gather(bf16[2,64,12,64]{3,1,2,0:T(8,128)(2,1)S(1)} %copy.154), channel_id=1, replica_groups=mesh['dp'=8,'seq'=4] {'seq'}, dimensions={1}, use_global_device_ids=true | all-gather | bytes 983040 | tf_op jit(solution)/shard_map/all_gather | solution.py:94
  404.9 54.9 %all_gather.88 = bf16[2,256,12,64]{3,0,2,1:T(2,128)(2,1)S(1)} all-gather(bf16[2,64,12,64]{3,0,2,1:T(2,128)(2,1)S(1)} %copy.159), channel_id=1, replica_groups=mesh['dp'=8,'seq'=4] {'seq'}, dimensions={1}, use_global_device_ids=true | all-gather | bytes 983040 | tf_op jit(solution)/shard_map/all_gather | solution.py:95
  463.8 40.0 %all_gather.77 = bf16[2,256,12,64]{3,0,2,1:T(2,128)(2,1)S(1)} all-gather(bf16[2,64,12,64]{3,0,2,1:T(2,128)(2,1)S(1)} %copy.153), channel_id=1, replica_groups=mesh['dp'=8,'seq'=4] {'seq'}, dimensions={1}, use_global_device_ids=true | all-gather | bytes 983040 | tf_op jit(solution)/shard_map/all_gather | solution.py:95
  508.6 4.6 fusion.24
  513.2 64.1 %all-gather.25.cloned.1.call-done = bf16[3072,768]{0,1:T(8,128)(2,1)} async-done(((bf16[3072,192]{0,1:T(8,128)(2,1)}), bf16[3072,768]{0,1:T(8,128)(2,1)}) %all-gather.25.cloned.1.call-update) | async-done | bytes 4718608 | tf_op jit(solution)/shard_map/all_gather | solution.py:291
  577.4 5.5 convert_reduce_fusion
  595.3 4.7 copy.198
  600.0 4.0 reshape.285
  604.6 4.5 fusion.21
  610.4 4.7 copy.200
  615.1 4.0 reshape.287
  619.1 5.6 convert_reduce_fusion.1
  628.2 4.7 fusion.76
  632.9 5.9 convert_reduce_fusion.6
  645.7 3.9 copy.194
  649.6 4.0 reshape.281
  670.8 5.1 reduce-scatter.43.cloned.1.call-done
  678.0 22.6 %reduce-scatter.45.cloned.1.call-done = bf16[64,1536]{1,0:T(8,128)(2,1)} async-done(((bf16[256,1536]{1,0:T(8,128)(2,1)}), bf16[64,1536]{1,0:T(8,128)(2,1)}) %reduce-scatter.45.cloned.1.call-update) | async-done | bytes 196624
  710.9 3.7 fusion
  717.4 3.8 fusion.1
  727.4 17.8 %all-reduce.12 = (bf16[2,4608]{1,0:T(2,128)(2,1)S(1)}, bf16[2,4608]{1,0:T(2,128)(2,1)S(1)}) all-reduce(bf16[2,4608]{1,0:T(2,128)(2,1)S(1)} %constant_dynamic-update-slice_fusion.6, bf16[2,4608]{1,0:T(2,128)(2,1)S(1)} %constant_dynamic-update-slice_fusion), channel_id=1, replica_groups=mesh['dp'=8,'seq'=4] {'seq'}, use_global_device_ids=true, to_apply=%region_39.40 | all-reduce | flops 18432 | bytes 73728 | tf_op jit(solution)/shard_map/psum | solution.py:241
  747.3 4.9 add_convert_fusion
  752.3 10.3 copy.202
  764.8 34.1 %reduce-scatter.31.cloned.1.call-done = bf16[768,576]{0,1:T(8,128)(2,1)} async-done(((bf16[768,2304]{0,1:T(8,128)(2,1)}), bf16[768,576]{0,1:T(8,128)(2,1)}) %reduce-scatter.31.cloned.1.call-update) | async-done | bytes 884752 | tf_op jit(solution)/shard_map/reduce_scatter | solution.py:344
  801.5 85.2 %reduce-scatter.39.cloned.1.call-done = bf16[3072,192]{0,1:T(8,128)(2,1)} async-done(((bf16[3072,768]{0,1:T(8,128)(2,1)}), bf16[3072,192]{0,1:T(8,128)(2,1)}) %reduce-scatter.39.cloned.1.call-update) | async-done | bytes 1179664 | tf_op jit(solution)/shard_map/reduce_scatter | solution.py:353
  889.7 85.0 %reduce-scatter.35.cloned.1.call-done = bf16[768,768]{1,0:T(8,128)(2,1)} async-done(((bf16[768,3072]{1,0:T(8,128)(2,1)}), bf16[768,768]{1,0:T(8,128)(2,1)}) %reduce-scatter.35.cloned.1.call-update) | async-done | bytes 1179664 | tf_op jit(solution)/shard_map/reduce_scatter | solution.py:350
  977.6 123.3 %reduce-scatter.51.cloned.1.call-done = bf16[1152,768]{1,0:T(8,128)(2,1)} async-done(((bf16[4608,768]{1,0:T(8,128)(2,1)}), bf16[1152,768]{1,0:T(8,128)(2,1)}) %reduce-scatter.51.cloned.1.call-update) | async-done | bytes 1769488
  1109.3 18.2 %all-reduce.11 = (bf16[4608]{0:T(1024)(128)(2,1)S(1)}, bf16[768]{0:T(1024)(128)(2,1)S(1)}, bf16[768]{0:T(1024)(128)(2,1)S(1)}, bf16[768]{0:T(1024)(128)(2,1)S(1)...) all-reduce(bf16[4608]{0:T(1024)(128)(2,1)S(1)} %add_convert_fusion., ...), channel_id=8, replica_groups=mesh['dp'=8,'seq'=4] {'seq'}, use_global_device_ids=true, to_apply=%region_44.45.clone | all-reduce | flops 10752 | bytes 43008
  1128.0 22.9 %all-reduce.10 = (f32[1152]{0:T(1024)}, f32[192]{0:T(256)}, f32[192]{0:T(256)}, f32[192]{0:T(256)}, f32[768]{0:T(1024)}, /*index=5*/f32[192]{0:T(256)}) all-reduce(f32[1152]{0:T(1024)S(1)} %dynamic-slice_convert_fusion, f32[192]{0:T(256)S(1)} %dynamic-slice_convert_fusion.5, ...), channel_id=1, replica_groups=mesh['dp'=8,'seq'=4] {'dp'}, use_global_device_ids=true, to_apply=%region_45.46 | all-reduce | flops 2688 | bytes 21504 | tf_op jit(solution)/shard_map/psum | solution.py:382
  1150.9 5.3 fusion.202
  1156.2 5.0 fusion.160
  1162.6 21.8 %reduce-scatter.53.cloned.1.call-done = f32[96,576]{1,0:T(8,128)} async-done(((f32[768,576]{1,0:T(8,128)}), f32[96,576]{1,0:T(8,128)}) %reduce-scatter.53.cloned.1.call-update) | async-done | bytes 221200
  1184.4 46.7 %reduce-scatter.41.cloned.1.call-done = f32[384,192]{0,1:T(8,128)} async-done(((f32[3072,192]{0,1:T(8,128)}), f32[384,192]{0,1:T(8,128)}) %reduce-scatter.41.cloned.1.call-update) | async-done | bytes 294928 | tf_op jit(solution)/shard_map/reduce_scatter | solution.py:380
  1231.0 46.4 %reduce-scatter.37.cloned.1.call-done = f32[96,768]{1,0:T(8,128)} async-done(((f32[768,768]{1,0:T(8,128)}), f32[96,768]{1,0:T(8,128)}) %reduce-scatter.37.cloned.1.call-update) | async-done | bytes 294928 | tf_op jit(solution)/shard_map/reduce_scatter | solution.py:379
  1277.5 52.6 %reduce-scatter.29.cloned.1.call-done = f32[96,1152]{1,0:T(8,128)} async-done(((f32[768,1152]{1,0:T(8,128)}), f32[96,1152]{1,0:T(8,128)}) %reduce-scatter.29.cloned.1.call-update) | async-done | bytes 442384 | tf_op jit(solution)/shard_map/reduce_scatter | solution.py:376
  (487 shorter events, 107.8 us)
Async XLA Ops:
  7.2 32.1 %copy-start.74 = (bf16[96,576]{1,0:T(8,128)(2,1)S(1)}, bf16[96,576]{1,0:T(8,128)(2,1)}, u32[]{:S(2)}) copy-start(bf16[96,576]{1,0:T(8,128)(2,1)} %param.18) | copy-start | bytes 331780
  7.2 32.0 %all-gather.11.cloned.1.call-start = ((), (), s32[]{:S(2)}) async-start(), calls=%async_computation.14 | async-start | bytes 1990656 | tf_op jit(solution)/shard_map/all_gather | solution.py:280
  7.9 57.2 %all-gather.19.cloned.1.call-start = ((), (), s32[]{:S(2)}) async-start(), calls=%async_computation.18 | async-start | bytes 1327104 | tf_op jit(solution)/shard_map/all_gather | solution.py:283
  8.7 98.0 %all-gather.23.cloned.1.call-start = ((), (), s32[]{:S(2)}) async-start(), calls=%async_computation.20 | async-start | bytes 1327104 | tf_op jit(solution)/shard_map/all_gather | solution.py:284
  9.4 211.5 %all-gather.13.cloned.1.call-start = ((), (), s32[]{:S(2)}) async-start(), calls=%async_computation.15 | async-start | bytes 8847360 | tf_op jit(solution)/shard_map/all_gather | solution.py:287
  39.2 251.3 %all-gather.15.cloned.1.call-start = ((), (), s32[]{:S(2)}) async-start(), calls=%async_computation.16 | async-start | bytes 4423680 | tf_op jit(solution)/shard_map/all_gather | solution.py:288
  51.3 28.6 %copy-start.128 = (bf16[1152]{0:T(1024)(128)(2,1)S(1)}, bf16[1152]{0:T(1024)(128)(2,1)}, u32[]{:S(2)}) copy-start(bf16[1152]{0:T(1024)(128)(2,1)} %param.17) | copy-start | bytes 6916
  51.4 54.9 %copy-start.14 = (bf16[2,2,64,768]{3,2,1,0:T(8,128)(2,1)S(1)}, bf16[2,2,64,768]{3,2,1,0:T(8,128)(2,1)}, u32[]{:S(2)}) copy-start(bf16[2,2,64,768]{3,2,1,0:T(8,128)(2,1)} %param.14) | copy-start | bytes 1179652
  51.4 410.5 %all-gather.17.cloned.1.call-start = ((), (), s32[]{:S(2)}) async-start(), calls=%async_computation.17 | async-start | bytes 1474560 | tf_op jit(solution)/shard_map/all_gather | solution.py:289
  61.1 447.5 %all-gather.21.cloned.1.call-start = ((), (), s32[]{:S(2)}) async-start(), calls=%async_computation.19 | async-start | bytes 5898240 | tf_op jit(solution)/shard_map/all_gather | solution.py:290
  65.1 155.7 %copy-start.100 = (bf16[2,2,768]{2,1,0:T(2,128)(2,1)S(1)}, bf16[2,2,768]{2,1,0:T(2,128)(2,1)}, u32[]{:S(2)}) copy-start(bf16[2,2,768]{2,1,0:T(2,128)(2,1)} %param.15) | copy-start | bytes 18436
  65.2 512.2 %all-gather.25.cloned.1.call-start = ((), (), s32[]{:S(2)}) async-start(), calls=%async_computation.21 | async-start | bytes 5898240 | tf_op jit(solution)/shard_map/all_gather | solution.py:291
  106.4 193.9 %copy-start.105 = (f32[2,64]{1,0:T(2,128)}, f32[2,64]{1,0:T(2,128)S(1)}, u32[]{:S(2)}) copy-start(f32[2,64]{1,0:T(2,128)S(1)} %broadcast_multiply_fusion.11) | copy-start | bytes 1540
  106.4 184.1 %copy-start.102 = (f32[2,64]{1,0:T(2,128)}, f32[2,64]{1,0:T(2,128)S(1)}, u32[]{:S(2)}) copy-start(f32[2,64]{1,0:T(2,128)S(1)} %broadcast_multiply_fusion.9) | copy-start | bytes 1540
  106.7 193.6 %copy-start.111 = (f32[2,64]{1,0:T(2,128)}, f32[2,64]{1,0:T(2,128)S(1)}, u32[]{:S(2)}) copy-start(f32[2,64]{1,0:T(2,128)S(1)} %add_rsqrt_fusion.3) | copy-start | bytes 1540
  106.7 183.8 %copy-start.108 = (f32[2,64]{1,0:T(2,128)}, f32[2,64]{1,0:T(2,128)S(1)}, u32[]{:S(2)}) copy-start(f32[2,64]{1,0:T(2,128)S(1)} %add_rsqrt_fusion.1) | copy-start | bytes 1540
  106.8 559.9 %reduce-scatter.47.cloned.1.call-start = ((), (), s32[]{:S(2)}) async-start(), calls=%async_computation.31 | async-start | bytes 983040
  224.9 68.9 %copy-start.71 = (f32[2,768]{1,0:T(2,128)}, f32[2,768]{1,0:T(2,128)S(1)}, u32[]{:S(2)}) copy-start(f32[2,768]{1,0:T(2,128)S(1)} %get-tuple-element.168) | copy-start | bytes 18436
  224.9 68.9 %copy-start.78 = (f32[2,768]{1,0:T(2,128)}, f32[2,768]{1,0:T(2,128)S(1)}, u32[]{:S(2)}) copy-start(f32[2,768]{1,0:T(2,128)S(1)} %get-tuple-element.167) | copy-start | bytes 18436
  224.9 280.1 %copy-start.91 = (f32[2,768]{1,0:T(2,128)}, f32[2,768]{1,0:T(2,128)S(1)}, u32[]{:S(2)}) copy-start(f32[2,768]{1,0:T(2,128)S(1)} %get-tuple-element.169) | copy-start | bytes 18436
  224.9 283.7 %copy-start.89 = (f32[2,768]{1,0:T(2,128)}, f32[2,768]{1,0:T(2,128)S(1)}, u32[]{:S(2)}) copy-start(f32[2,768]{1,0:T(2,128)S(1)} %get-tuple-element.165) | copy-start | bytes 18436
  225.0 352.4 %copy-start.114 = (f32[2,768]{1,0:T(2,128)}, f32[2,768]{1,0:T(2,128)S(1)}, u32[]{:S(2)}) copy-start(f32[2,768]{1,0:T(2,128)S(1)} %get-tuple-element.164) | copy-start | bytes 18436
  294.6 52.2 %copy-start.31 = (bf16[2,64,768]{1,2,0:T(8,128)(2,1)}, bf16[2,64,768]{1,2,0:T(8,128)(2,1)S(1)}, u32[]{:S(2)}) copy-start(bf16[2,64,768]{1,2,0:T(8,128)(2,1)S(1)} %copy.209) | copy-start | bytes 589828
  300.2 204.8 %copy-start.118 = (f32[2,768]{1,0:T(2,128)}, f32[2,768]{1,0:T(2,128)S(1)}, u32[]{:S(2)}) copy-start(f32[2,768]{1,0:T(2,128)S(1)} %get-tuple-element.163) | copy-start | bytes 18436
  302.9 100.3 %copy-start.29 = (bf16[2,64,768]{1,2,0:T(8,128)(2,1)}, bf16[2,64,768]{1,2,0:T(8,128)(2,1)S(1)}, u32[]{:S(2)}) copy-start(bf16[2,64,768]{1,2,0:T(8,128)(2,1)S(1)} %copy.208) | copy-start | bytes 589828
  348.0 111.7 %copy-start = (f32[2,12,64,256]{3,2,1,0:T(8,128)}, f32[2,12,64,256]{3,2,1,0:T(8,128)S(1)}, u32[]{:S(2)}) copy-start(f32[2,12,64,256]{3,2,1,0:T(8,128)S(1)} %get-tuple-element.177) | copy-start | bytes 4718596
  404.9 99.0 %copy-start.87 = (f32[2,12,64]{2,1,0:T(8,128)}, f32[2,12,64]{2,1,0:T(8,128)S(1)}, u32[]{:S(2)}) copy-start(f32[2,12,64]{2,1,0:T(8,128)S(1)} %fusion.54) | copy-start | bytes 18436
  463.8 41.3 %copy-start.39 = (f32[2,64,768]{2,1,0:T(8,128)}, f32[2,64,768]{2,1,0:T(8,128)S(1)}, u32[]{:S(2)}) copy-start(f32[2,64,768]{2,1,0:T(8,128)S(1)} %convolution_add_fusion.4) | copy-start | bytes 1179652
  507.0 78.3 %copy-start.82 = (f32[2,64]{1,0:T(2,128)}, f32[2,64]{1,0:T(2,128)S(1)}, u32[]{:S(2)}) copy-start(f32[2,64]{1,0:T(2,128)S(1)} %broadcast_multiply_fusion.8) | copy-start | bytes 1540
  508.0 75.0 %copy-start.95 = (f32[2,64]{1,0:T(2,128)}, f32[2,64]{1,0:T(2,128)S(1)}, u32[]{:S(2)}) copy-start(f32[2,64]{1,0:T(2,128)S(1)} %add_rsqrt_fusion) | copy-start | bytes 1540
  508.6 74.3 %slice-start = ((s8[4718592]{0:T(1024)(128)(4,1)}), s8[524288]{0:T(1024)(128)(4,1)S(1)}, s32[]{:S(2)}) async-start(s8[4718592]{0:T(1024)(128)(4,1)} %bitcast.349), calls=%async_computation.36 | async-start | bytes 1048576
  604.1 64.7 %reduce-scatter.49.cloned.1.call-start = ((), (), s32[]{:S(2)}) async-start(), calls=%async_computation.32 | async-start | bytes 983040
  627.9 48.1 %reduce-scatter.43.cloned.1.call-start = ((), (), s32[]{:S(2)}) async-start(), calls=%async_computation.29 | async-start | bytes 983040
  653.6 47.0 %reduce-scatter.45.cloned.1.call-start = ((), (), s32[]{:S(2)}) async-start(), calls=%async_computation.30 | async-start | bytes 983040
  659.5 103.1 %reduce-scatter.33.cloned.1.call-start = ((), (), s32[]{:S(2)}) async-start(), calls=%async_computation.24 | async-start | bytes 1474560 | tf_op jit(solution)/shard_map/reduce_scatter | solution.py:347
  662.1 136.8 %reduce-scatter.31.cloned.1.call-start = ((), (), s32[]{:S(2)}) async-start(), calls=%async_computation.23 | async-start | bytes 4423680 | tf_op jit(solution)/shard_map/reduce_scatter | solution.py:344
  664.5 38.2 %copy-start.63 = (bf16[2,64,768]{2,1,0:T(8,128)(2,1)}, bf16[2,64,768]{2,1,0:T(8,128)(2,1)S(1)}, u32[]{:S(2)}) copy-start(bf16[2,64,768]{2,1,0:T(8,128)(2,1)S(1)} %copy.171) | copy-start | bytes 589828
  666.6 37.4 %copy-start.59 = (bf16[2,64,768]{2,1,0:T(8,128)(2,1)}, bf16[2,64,768]{2,1,0:T(8,128)(2,1)S(1)}, u32[]{:S(2)}) copy-start(bf16[2,64,768]{2,1,0:T(8,128)(2,1)S(1)} %copy.179) | copy-start | bytes 589828
  668.7 35.3 %copy-start.60 = (bf16[2,64,768]{2,1,0:T(8,128)(2,1)}, bf16[2,64,768]{2,1,0:T(8,128)(2,1)S(1)}, u32[]{:S(2)}) copy-start(bf16[2,64,768]{2,1,0:T(8,128)(2,1)S(1)} %copy.192) | copy-start | bytes 589828
  670.8 33.2 %copy-start.45 = (bf16[2,64,768]{2,1,0:T(8,128)(2,1)}, bf16[2,64,768]{2,1,0:T(8,128)(2,1)S(1)}, u32[]{:S(2)}) copy-start(bf16[2,64,768]{2,1,0:T(8,128)(2,1)S(1)} %copy.193) | copy-start | bytes 589828
  707.1 179.6 %reduce-scatter.39.cloned.1.call-start = ((), (), s32[]{:S(2)}) async-start(), calls=%async_computation.27 | async-start | bytes 5898240 | tf_op jit(solution)/shard_map/reduce_scatter | solution.py:353
  714.7 260.0 %reduce-scatter.35.cloned.1.call-start = ((), (), s32[]{:S(2)}) async-start(), calls=%async_computation.25 | async-start | bytes 5898240 | tf_op jit(solution)/shard_map/reduce_scatter | solution.py:350
  721.2 379.7 %reduce-scatter.51.cloned.1.call-start = ((), (), s32[]{:S(2)}) async-start(), calls=%async_computation.33 | async-start | bytes 8847360
  762.6 400.0 %reduce-scatter.55.cloned.1.call-start = ((), (), s32[]{:S(2)}) async-start(), calls=%async_computation.35 | async-start | bytes 884736
  764.7 419.7 %reduce-scatter.53.cloned.1.call-start = ((), (), s32[]{:S(2)}) async-start(), calls=%async_computation.34 | async-start | bytes 2211840
  801.4 429.6 %reduce-scatter.41.cloned.1.call-start = ((), (), s32[]{:S(2)}) async-start(), calls=%async_computation.28 | async-start | bytes 2654208 | tf_op jit(solution)/shard_map/reduce_scatter | solution.py:380
  889.7 387.8 %reduce-scatter.37.cloned.1.call-start = ((), (), s32[]{:S(2)}) async-start(), calls=%async_computation.26 | async-start | bytes 2654208 | tf_op jit(solution)/shard_map/reduce_scatter | solution.py:379
  977.6 352.4 %reduce-scatter.29.cloned.1.call-start = ((), (), s32[]{:S(2)}) async-start(), calls=%async_computation.22 | async-start | bytes 3981312 | tf_op jit(solution)/shard_map/reduce_scatter | solution.py:376
  (118 other events, 527.6 us)
Sparse Core Ops, SparseCore 0:
  9.9 29.2 all-gather.10
  41.0 24.0 all-gather.18
  67.0 24.1 all-gather.22
  92.6 128.2 all-gather.12
  222.3 68.1 all-gather.14
  292.5 44.1 all-gather.16
  338.3 146.2 all-gather.20
  486.2 91.1 all-gather.24
  604.2 22.0 reduce-scatter.46
  628.4 22.5 reduce-scatter.48
  653.8 22.1 reduce-scatter.42
  678.1 22.5 reduce-scatter.44
  703.0 28.4 reduce-scatter.32
  733.7 65.2 reduce-scatter.30
  801.1 85.6 reduce-scatter.38
  888.9 85.7 reduce-scatter.34
  976.8 124.0 reduce-scatter.50
  1104.5 35.5 reduce-scatter.54
  1144.0 40.3 reduce-scatter.52
  1188.5 42.4 reduce-scatter.40
  1235.0 42.4 reduce-scatter.36
  1281.9 48.0 reduce-scatter.28
where the time goes:
time: 1350 us; the launch traced here: 1340 us
  waiting for transfers between devices  803 us (59%)
  blocking collectives  309 us (23%)
  matrix products  108 us (8%)
  local copies, waits for them, and re-layouts  77.9 us (6%)
  between operations  19.5 us (1%)
  other arithmetic  18.5 us (1%)
    unnamed x29, waiting for transfers between devices  175 us
    all_gather x1, waiting for transfers between devices, local(): lax.all_gather(rows[0], 'seq', axis=1, tiled=True)  114 us
    all_gather x2, blocking collectives, forward_micro(): lax.all_gather(keys, 'seq', axis=1, tiled=True)  97.8 us
    all_gather x2, blocking collectives, forward_micro(): lax.all_gather(values, 'seq', axis=1, tiled=True)  94.9 us
    reduce_scatter x1, waiting for transfers between devices, local(): lax.psum_scatter(accumulated[9].astype(jnp.bfloat16), 'seq', scatter_dime...  85.2 us
    reduce_scatter x1, waiting for transfers between devices, local(): lax.psum_scatter(accumulated[7].astype(jnp.bfloat16), 'seq', scatter_dime...  85 us
    unnamed x330, local copies, waits for them, and re-layouts  69.6 us
    all_gather x1, waiting for transfers between devices, local(): lax.all_gather(rows[1], 'seq', axis=1, tiled=True)  65.5 us
  transfers between devices with their start and end apart: 22, of which 15 were waited for; matrix products, arithmetic and copies ran while one was open for 12% of the time, Pallas kernels for 0%

commit v1 on v0

v1 whole, which is shorter than its diff:
```python
import jax
import jax.numpy as jnp
from jax import lax
from jax.sharding import PartitionSpec as P

H = 12
EPSILON = 1e-06
BF = jnp.bfloat16
F32 = jnp.float32


def bits_of(count):
    bits = count.bit_length() - 1
    assert 1 << bits == count
    return bits


def swap(values, axis, bit):
    count = lax.axis_size(axis)
    return lax.ppermute(values, axis, [(i, i ^ (1 << bit)) for i in range(count)])


def own_bit(axis, bit):
    return (lax.axis_index(axis) >> bit) & 1


def join(values, axis, bit):
    other = swap(values, axis, bit)
    mine = own_bit(axis, bit) == 0
    return jnp.stack([jnp.where(mine, values, other), jnp.where(mine, other, values)])


def halve(values, axis, bit):
    index = own_bit(axis, bit)
    sent = lax.dynamic_index_in_dim(values, 1 - index, 0, keepdims=False)
    kept = lax.dynamic_index_in_dim(values, index, 0, keepdims=False)
    other = swap(sent.astype(BF), axis, bit)
    return kept.astype(F32) + other.astype(F32)


def gather_seq(values):
    count = bits_of(lax.axis_size("seq"))
    shape = values.shape
    order = list(range(count - 1, -1, -1))
    for bit in order:
        values = join(values, "seq", bit)
    values = values.transpose(list(range(count - 1, -1, -1)) + list(range(count, count + len(shape))))
    return values.reshape((1 << count,) + shape)


def scatter_seq(values):
    count = bits_of(lax.axis_size("seq"))
    shape = values.shape[1:]
    values = values.reshape((2,) * count + shape)
    values = values.transpose(list(range(count - 1, -1, -1)) + list(range(count, count + len(shape))))
    for bit in range(count):
        values = halve(values, "seq", bit)
    return values


def dp_orders():
    count = bits_of(lax.axis_size("dp"))
    upper = list(range(1, count))
    return (upper + [0], upper[::-1] + [0])


def gather_dp(units):
    count = bits_of(lax.axis_size("dp"))
    half = units.shape[-1] // 2
    parts = []
    for part, order in zip((units[..., :half], units[..., half:]), dp_orders()):
        for bit in order:
            part = join(part, "dp", bit)
        dims = [order[::-1].index(bit) for bit in range(count - 1, -1, -1)]
        part = part.transpose(dims + [count, count + 1, count + 2])
        parts.append(part.reshape((1 << count,) + part.shape[count:]))
    return jnp.concatenate(parts, axis=-1)


def scatter_dp(grads):
    count = bits_of(lax.axis_size("dp"))
    half = grads.shape[-1] // 2
    parts = []
    for part, order in zip((grads[..., :half], grads[..., half:]), dp_orders()):
        back = order[::-1]
        part = part.reshape((2,) * count + part.shape[1:])
        dims = [count - 1 - bit for bit in back]
        part = part.transpose(dims + [count, count + 1, count + 2])
        for bit in back:
            part = halve(part, "dp", bit)
        parts.append(part)
    return jnp.concatenate(parts, axis=-1)


def normalize(values):
    center = values - jnp.mean(values, axis=-1, keepdims=True)
    inverse = lax.rsqrt(jnp.mean(center * center, axis=-1, keepdims=True) + EPSILON)
    return (center * inverse, inverse)


def norm_back(grad_normed, normed, inverse):
    first = jnp.mean(grad_normed, axis=-1, keepdims=True)
    second = jnp.mean(grad_normed * normed, axis=-1, keepdims=True)
    return inverse * (grad_normed - first - normed * second)


def project(values, matrix):
    return jnp.einsum("lsd,dn->lsn", values, matrix, preferred_element_type=F32)


def project_back(grads, matrix):
    return jnp.einsum("lsn,dn->lsd", grads, matrix, preferred_element_type=F32)


def outer_sum(values, grads):
    return jnp.einsum("lsd,lsn->dn", values, grads, preferred_element_type=F32)


def column_sum(grads):
    return jnp.sum(grads.astype(F32), axis=(0, 1))


def gelu_tanh(values):
    return jax.nn.gelu(values, approximate=True)


def local(
    latents,
    conditions,
    modulator,
    modbias,
    qkvweight,
    querybias,
    valuebias,
    projection,
    projbias,
    expand,
    expandbias,
    contract,
    contractbias,
    cotangent,
):
    n_dp, n_seq = lax.axis_size("dp"), lax.axis_size("seq")
    micro, lats, tok, width = latents.shape
    held = micro * lats
    assert held % n_seq == 0
    own = held // n_seq
    rows = width // n_dp
    chunk = width // n_seq
    wide = contract.shape[0] // rows
    head = width // H
    factor = head ** (-0.5)

    g1 = gather_seq(jnp.concatenate([qkvweight, projection], axis=1))
    g2 = gather_seq(expand)
    g3 = gather_seq(contract)
    u_qkv = g1[:, :, : 3 * chunk].transpose(1, 0, 2).reshape(rows, 3, width).transpose(1, 0, 2)
    u_proj = g1[:, :, 3 * chunk :].transpose(1, 0, 2).reshape(1, rows, width)
    u1 = jnp.concatenate([u_qkv, u_proj], axis=0)
    u2 = g2.transpose(1, 0, 2).reshape(rows, wide, width).transpose(1, 0, 2)
    u3 = g3.transpose(1, 0, 2).reshape(wide, rows, width)
    w1 = gather_dp(u1)
    w2 = gather_dp(u2)
    w3 = gather_dp(u3)
    qkv_matrix = w1[:, :3].transpose(0, 2, 1, 3).reshape(width, 3 * width)
    proj_matrix = w1[:, 3].reshape(width, width)
    up_matrix = w2.transpose(0, 2, 1, 3).reshape(width, wide * width)
    down_matrix = w3.reshape(wide * width, width)

    biases = (querybias, valuebias, projbias, expandbias, contractbias)
    gathered = gather_seq(jnp.concatenate(biases))
    sizes = [b.shape[0] for b in biases]
    starts = [sum(sizes[:i]) for i in range(len(sizes))]
    query_offset, value_offset, proj_offset, up_offset, down_offset = [
        gathered[:, a : a + n].reshape(-1).astype(F32) for a, n in zip(starts, sizes)
    ]

    def to_latents(values):
        values = values.reshape(held, tok, width)
        return lax.all_to_all(values, "seq", 0, 1, tiled=True)

    def to_tokens(values):
        values = lax.all_to_all(values, "seq", 1, 0, tiled=True)
        return values.reshape(micro, lats, tok, width)

    tokens = to_latents(latents).astype(F32)
    dout = to_latents(cotangent).astype(F32)

    cond_float = conditions.reshape(held, width).astype(F32)
    cond_act = jax.nn.silu(cond_float).astype(BF)
    cond_rows = lax.all_to_all(
        cond_act.reshape(held, n_dp, rows), "dp", 1, 0, tiled=True
    ).reshape(n_dp * held, rows)
    part = jnp.dot(cond_rows, modulator, preferred_element_type=F32)
    part = lax.all_to_all(part.reshape(n_dp, held, -1), "dp", 0, 0, tiled=True)
    piece = jnp.sum(part, axis=0) + modbias.astype(F32)
    modulation = lax.all_to_all(piece, "seq", 0, 1, tiled=True)
    pieces = jnp.split(modulation[:, None, :], 6, axis=-1)

    normed1, inverse1 = normalize(tokens)
    hidden1 = (normed1 * (1.0 + pieces[1]) + pieces[0]).astype(BF)
    offsets = jnp.concatenate([query_offset, jnp.zeros_like(query_offset), value_offset])
    qkv_low = (project(hidden1, qkv_matrix) + offsets).astype(BF)
    length = qkv_low.shape[1]
    queries = qkv_low[..., :width].reshape(own, length, H, head)
    keys = qkv_low[..., width : 2 * width].reshape(own, length, H, head)
    values = qkv_low[..., 2 * width :].reshape(own, length, H, head)
    scores = jnp.einsum("lshd,lthd->lhst", queries, keys, preferred_element_type=F32) * factor
    highest = jnp.max(scores, axis=-1, keepdims=True)
    expo = jnp.exp(scores - highest)
    totals = jnp.sum(expo, axis=-1, keepdims=True)
    probs = expo / totals
    probs_low = probs.astype(BF)
    attended = jnp.einsum("lhst,lthd->lshd", probs_low, values, preferred_element_type=F32)
    attended = attended.reshape(own, length, width).astype(BF)
    branch1 = project(attended, proj_matrix) + proj_offset
    middle = tokens + pieces[2] * branch1
    normed2, inverse2 = normalize(middle)
    hidden2 = (normed2 * (1.0 + pieces[4]) + pieces[3]).astype(BF)
    before = project(hidden2, up_matrix) + up_offset
    active = gelu_tanh(before).astype(BF)
    branch2 = project(active, down_matrix) + down_offset
    result = to_tokens((middle + pieces[5] * branch2).astype(BF))

    dbranch2 = (pieces[5] * dout).astype(BF)
    dgate2 = jnp.sum(dout * branch2, axis=1)
    grad_down = outer_sum(active, dbranch2).astype(BF)
    grad_down_offset = column_sum(dbranch2)
    s3 = scatter_dp(grad_down.reshape(n_dp, wide, rows, width))
    dactive = project_back(dbranch2, down_matrix)
    dbefore = jax.vjp(gelu_tanh, before)[1](dactive)[0].astype(BF)
    grad_up = outer_sum(hidden2, dbefore).astype(BF)
    grad_up_offset = column_sum(dbefore)
    s2 = scatter_dp(grad_up.reshape(n_dp, rows, wide, width).transpose(0, 2, 1, 3))
    dhidden2 = project_back(dbefore, up_matrix)
    dshift2 = jnp.sum(dhidden2, axis=1)
    dscale2 = jnp.sum(dhidden2 * normed2, axis=1)
    dmiddle = dout + norm_back(dhidden2 * (1.0 + pieces[4]), normed2, inverse2)
    dbranch1 = (pieces[2] * dmiddle).astype(BF)
    dgate1 = jnp.sum(dmiddle * branch1, axis=1)
    grad_proj = outer_sum(attended, dbranch1).astype(BF)
    grad_proj_offset = column_sum(dbranch1)
    dattended = project_back(dbranch1, proj_matrix).astype(BF)
    dattended = dattended.reshape(own, length, H, head)
    dprobs = jnp.einsum("lshd,lthd->lhst", dattended, values, preferred_element_type=F32)
    rowsum = jnp.sum(dprobs * probs, axis=-1, keepdims=True)
    dscores = (probs * (dprobs - rowsum)).astype(BF)
    dqueries = jnp.einsum("lhst,lthd->lshd", dscores, keys, preferred_element_type=F32) * factor
    dkeys = jnp.einsum("lhst,lshd->lthd", dscores, queries, preferred_element_type=F32) * factor
    dvalues = jnp.einsum("lhst,lshd->lthd", probs_low, dattended, preferred_element_type=F32)
    dqkv = jnp.concatenate(
        [part.reshape(own, length, width) for part in (dqueries, dkeys, dvalues)], axis=-1
    ).astype(BF)
    grad_qkv = outer_sum(hidden1, dqkv).astype(BF)
    grad_query_offset = column_sum(dqkv[..., :width])
    grad_value_offset = column_sum(dqkv[..., 2 * width :])
    grad1 = jnp.concatenate([grad_qkv, grad_proj], axis=1)
    s1 = scatter_dp(grad1.reshape(n_dp, rows, 4, width).transpose(0, 2, 1, 3))
    dhidden1 = project_back(dqkv, qkv_matrix)
    dshift1 = jnp.sum(dhidden1, axis=1)
    dscale1 = jnp.sum(dhidden1 * normed1, axis=1)
    dtokens = dmiddle + norm_back(dhidden1 * (1.0 + pieces[1]), normed1, inverse1)
    token_grad = to_tokens(dtokens.astype(BF))

    dmod = jnp.concatenate([dshift1, dscale1, dgate1, dshift2, dscale2, dgate2], axis=-1)
    offset_grads = (
        grad_query_offset, grad_value_offset, grad_proj_offset, grad_up_offset, grad_down_offset
    )
    offset_grads = jnp.concatenate([g.reshape(n_seq, -1) for g in offset_grads], axis=1)
    dmod_cols = dmod.reshape(own, n_seq, -1).transpose(1, 0, 2).reshape(n_seq, -1)
    small = jnp.concatenate([dmod_cols, offset_grads], axis=1).astype(BF)
    small = lax.all_to_all(small, "seq", 0, 0, tiled=True)
    small = lax.all_gather(small, "dp", axis=0, tiled=True)
    cols = modulator.shape[1]
    dmod_all = small[:, : own * cols].reshape(n_dp * held, cols)
    offset_sums = jnp.sum(small[:, own * cols :].astype(F32), axis=0)
    grad_mod = jnp.einsum("ld,ln->dn", cond_rows, dmod_all, preferred_element_type=F32)
    grad_mod_offset = jnp.sum(dmod_all.astype(F32), axis=0)
    dcond_rows = jnp.einsum("ln,dn->ld", dmod_all, modulator, preferred_element_type=F32)
    dcond = lax.all_to_all(dcond_rows.reshape(n_dp, held, rows), "dp", 0, 2, tiled=True)
    dcond = dcond.reshape(held, width)
    for bit in range(bits_of(n_seq)):
        dcond = dcond + swap(dcond, "seq", bit)
    dconds = jax.vjp(jax.nn.silu, cond_float)[1](dcond)[0].reshape(micro, lats, width)

    t1 = jnp.concatenate([s1[u] for u in range(3)], axis=1).reshape(rows, n_seq, 3 * chunk)
    t1 = jnp.concatenate([t1, s1[3].reshape(rows, n_seq, chunk)], axis=2).transpose(1, 0, 2)
    t2 = s2.transpose(1, 0, 2).reshape(rows, n_seq, -1).transpose(1, 0, 2)
    t3 = s3.reshape(wide * rows, n_seq, chunk).transpose(1, 0, 2)
    r3 = scatter_seq(t3)
    r2 = scatter_seq(t2)
    r1 = scatter_seq(t1)
    sums = [offset_sums[a : a + n] for a, n in zip(starts, sizes)]
    return (
        result,
        token_grad,
        dconds,
        grad_mod,
        grad_mod_offset,
        r1[:, : 3 * chunk],
        sums[0],
        sums[1],
        r1[:, 3 * chunk :],
        sums[2],
        r2,
        sums[3],
        r3,
        sums[4],
    )


def solution(mesh):
    placed = (
        P(None, "dp", "seq", None),
        P(None, "dp", None),
        P("dp", "seq"),
        P("seq"),
        P("dp", "seq"),
        P("seq"),
        P("seq"),
        P("dp", "seq"),
        P("seq"),
        P("dp", "seq"),
        P("seq"),
        P("dp", "seq"),
        P("seq"),
        P(None, "dp", "seq", None),
    )
    return jax.shard_map(
        local,
        mesh=mesh,
        in_specs=placed,
        out_specs=(
            P(None, "dp", "seq", None),
            P(None, "dp", "seq", None),
            P(None, "dp", None),
            P("dp", "seq"),
            P("seq"),
            P("dp", "seq"),
            P("seq"),
            P("seq"),
            P("dp", "seq"),
            P("seq"),
            P("dp", "seq"),
            P("seq"),
            P("dp", "seq"),
            P("seq"),
        ),
        check_vma=False,
    )
```

time: 1350 us -> 575 us (0.43)
  waiting for transfers between devices: 803 us -> 91.6 us
  blocking collectives: 309 us -> 8.71 us
  local copies, waits for them, and re-layouts: 77.9 us -> 207 us
  other arithmetic: 18.5 us -> 114 us
  starting transfers between devices: 1.93 us -> 96.1 us
  matrix products: 108 us -> 47.2 us
  between operations: 19.5 us -> 2.26 us
    reduce_scatter x7 -> x0, waiting for transfers between devices: 350 us -> none  [the longest x1 85.2 us: local(): lax.psum_scatter(accumulated[9].astype(jnp.bfloat16), 'seq', scatter_dime...]
    all_gather x8 -> x0, waiting for transfers between devices: 277 us -> none  [the longest x1 114 us: local(): lax.all_gather(rows[0], 'seq', axis=1, tiled=True)]
    all_gather x8 -> x1, blocking collectives: 238 us -> 8.71 us  [local(): small = lax.all_gather(small, 'dp', axis=0, tiled=True)]
    unnamed x29 -> x0, waiting for transfers between devices: 175 us -> none
    ppermute x0 -> x52, waiting for transfers between devices: none -> 78.1 us  [swap(): return lax.ppermute(values, axis, [(i, i ^ 1 << bit) for i in range(count)])]
    dot_general x42 -> x20, matrix products: 108 us -> 43.2 us  [the longest x4 13.9 us: outer_sum(): return jnp.einsum('lsd,lsn->dn', values, grads, preferred_element_type=F32)]
    ppermute x0 -> x52, starting transfers between devices: none -> 58.6 us  [swap(): return lax.ppermute(values, axis, [(i, i ^ 1 << bit) for i in range(count)])]
    another operation x3 -> x41, other arithmetic: 2.18 us -> 46.3 us  [join(): jnp.stack([jnp.where(mine, values, other), jnp.where(mine, other, values)])]
  transfers between devices with their start and end apart: 22 -> 61, of which waited for: 15 -> 20; matrix products, arithmetic and copies ran while one was open for 12% -> 45% of each run, Pallas kernels for 0% -> 0%
where the time goes in v1:
time: 575 us; the launch traced here: 566 us
  local copies, waits for them, and re-layouts  207 us (36%)
  other arithmetic  114 us (20%)
  starting transfers between devices  96.1 us (17%)
  waiting for transfers between devices  91.6 us (16%)
  matrix products  47.2 us (8%)
  blocking collectives  8.71 us (2%)
    ppermute x52, waiting for transfers between devices, swap(): return lax.ppermute(values, axis, [(i, i ^ 1 << bit) for i in range(count)])  78.1 us
    ppermute x52, starting transfers between devices, swap(): return lax.ppermute(values, axis, [(i, i ^ 1 << bit) for i in range(count)])  58.6 us
    another operation x41, other arithmetic, join(): jnp.stack([jnp.where(mine, values, other), jnp.where(mine, other, values)])  46.3 us
    unnamed x163, local copies, waits for them, and re-layouts  29.2 us
    ppermute x12, local copies, waits for them, and re-layouts, swap(): return lax.ppermute(values, axis, [(i, i ^ 1 << bit) for i in range(count)])  28.8 us
    another operation x14, local copies, waits for them, and re-layouts, join(): jnp.stack([jnp.where(mine, values, other), jnp.where(mine, other, values)])  27.5 us
    transpose x6, local copies, waits for them, and re-layouts, gather_dp(): part = part.transpose(dims + [count, count + 1, count + 2])  25.2 us
    transpose x6, other arithmetic, gather_dp(): part = part.transpose(dims + [count, count + 1, count + 2])  19 us
  transfers between devices with their start and end apart: 61, of which 20 were waited for; matrix products, arithmetic and copies ran while one was open for 45% of the time, Pallas kernels for 0%

profile of v1, /device:TPU:0, one launch (start us, length us, event | category | flops | bytes accessed | tf_op | source)
XLA Modules:
  0.0 566.5 jit_solution(18030800586894622624)
XLA Ops:
  0.7 3.5 concatenate.99
  4.2 4.0 collective-permute-start.8
  9.6 3.7 all-to-all-start.1
  22.8 4.2 all-to-all-start.2
  27.6 5.1 all-to-all-done.2
  33.4 3.9 all-to-all-start.3
  43.4 3.6 all-to-all-start
  49.9 7.1 %collective-permute-done.19 = bf16[2,384,192]{1,2,0:T(8,128)(2,1)S(1)} collective-permute-done((bf16[2,384,192]{1,2,0:T(8,128)(2,1)S(1)}, bf16[2,384,192]{1,2,0:T(8,128)(2,1)S(1)}, u32[]{:S(2)}, u32[]{:S(2)}) %collective-permute-start.19) | collective-permute-done | bytes 294944 | tf_op jit(solution)/shard_map/ppermute | solution.py:20
  58.8 5.4 collective-permute-done.11
  75.1 4.5 all-to-all-start.5
  80.2 8.3 %all-to-all-done.5 = bf16[4,64,768]{2,1,0:T(8,128)(2,1)S(1)} async-done(((bf16[4,64,768]{2,1,0:T(8,128)(2,1)}), bf16[4,64,768]{2,1,0:T(8,128)(2,1)S(1)}, u32[]{:S(2)}, u32[]{:S(2)}) %all-to-all-start.5) | async-done | bytes 393248 | tf_op jit(solution)/shard_map/all_to_all | solution.py:180
  97.9 7.2 %collective-permute-done.5 = bf16[4,96,384]{1,2,0:T(8,128)(2,1)} collective-permute-done((bf16[4,96,384]{1,2,0:T(8,128)(2,1)}, bf16[4,96,384]{1,2,0:T(8,128)(2,1)}, u32[]{:S(2)}, u32[]{:S(2)}) %collective-permute-start.5) | collective-permute-done | bytes 294944 | tf_op jit(solution)/shard_map/ppermute | solution.py:20
  139.4 3.5 collective-permute-done.24
  201.2 4.8 select_bitcast_fusion.1
  208.6 4.4 maximum_bitcast_fusion.6
  218.9 4.5 copy.305
  223.4 4.5 copy.286
  227.9 3.8 maximum_bitcast_fusion.2
  242.3 4.5 copy.256
  258.0 5.0 copy.278
  265.4 3.6 copy.287
  272.2 6.8 %copy.264 = bf16[8,96,3,768]{1,0,3,2:T(8,128)(2,1)} copy(bf16[8,96,3,768]{3,1,2,0:T(8,128)(2,1)} %fusion.4) | data formatting | bytes 7077888 | tf_op jit(solution)/shard_map/transpose | solution.py:165
  279.0 8.3 %reshape.935 = bf16[768,2304]{0,1:T(8,128)(2,1)} reshape(bf16[8,96,3,768]{1,0,3,2:T(8,128)(2,1)} %copy.264) | data formatting | bytes 7077888 | tf_op jit(solution)/shard_map/reshape | solution.py:165
  295.0 3.8 maximum_bitcast_fusion.5
  302.2 4.0 fusion.102
  312.1 3.5 fusion.103
  323.4 4.4 convolution_convert_fusion
  327.9 3.8 convolution_convert_fusion.1
  331.8 3.4 bitcast_reduce_fusion
  352.0 9.8 %reshape.959 = bf16[8,96,4,768]{3,2,1,0:T(4,128)(2,1)} reshape(bf16[768,3072]{1,0:T(8,128)(2,1)} %convolution_convert_fusion.1) | data formatting | bytes 9437184 | tf_op jit(solution)/shard_map/reshape | solution.py:234
  367.4 3.7 fusion.36
  374.2 3.4 all-to-all-start.7
  377.7 4.2 convolution_convert_fusion.2
  385.3 8.7 %all-gather = bf16[32,1,2688]{2,1,0:T(2,128)(2,1)S(1)} all-gather(bf16[4,1,2688]{2,1,0:T(2,128)(2,1)S(1)} %reshape.1006), channel_id=2, replica_groups=mesh['dp'=8,'seq'=4] {'dp'}, dimensions={0}, use_global_device_ids=true | all-gather | bytes 193536 | tf_op jit(solution)/shard_map/all_gather | solution.py:273
  394.9 3.7 all-to-all-start.8
  398.6 5.1 pad_maximum_fusion.1
  403.7 9.7 %reshape.954 = bf16[8,96,4,768]{3,2,1,0:T(4,128)(2,1)} reshape(bf16[768,3072]{1,0:T(8,128)(2,1)} %pad_maximum_fusion.1) | data formatting | bytes 9437184 | tf_op jit(solution)/shard_map/reshape | solution.py:258
  413.5 5.4 copy.376
  418.8 5.1 all-to-all-start.4
  423.9 5.3 fusion.97
  429.8 3.9 reduce.69
  442.8 5.3 all-to-all-start.6
  450.8 4.5 collective-permute-done.26
  455.3 4.1 collective-permute-start.27
  491.5 7.5 %collective-permute-done.37 = bf16[2,4,96,384]{3,2,1,0:T(8,128)(2,1)S(1)} collective-permute-done((bf16[2,4,96,384]{3,2,1,0:T(8,128)(2,1)S(1)}, bf16[2,4,96,384]{3,2,1,0:T(8,128)(2,1)S(1)}, u32[]{:S(2)}, u32[]{:S(2)}) %collective-permute-start.37) | collective-permute-done | bytes 589856 | tf_op jit(solution)/shard_map/ppermute | solution.py:20
  505.0 10.2 %collective-permute-done.32 = bf16[2,4,96,384]{3,2,1,0:T(8,128)(2,1)S(1)} collective-permute-done((bf16[2,4,96,384]{3,2,1,0:T(8,128)(2,1)S(1)}, bf16[2,4,96,384]{3,2,1,0:T(8,128)(2,1)S(1)}, u32[]{:S(2)}, u32[]{:S(2)}) %collective-permute-start.32) | collective-permute-done | bytes 589856 | tf_op jit(solution)/shard_map/ppermute | solution.py:20
  543.3 7.4 %collective-permute-done.34 = bf16[2,96,768]{2,1,0:T(8,128)(2,1)S(1)} collective-permute-done((bf16[2,96,768]{2,1,0:T(8,128)(2,1)S(1)}, bf16[2,96,768]{2,1,0:T(8,128)(2,1)S(1)}, u32[]{:S(2)}, u32[]{:S(2)}) %collective-permute-start.34) | collective-permute-done | bytes 294944 | tf_op jit(solution)/shard_map/ppermute | solution.py:20
  554.9 7.9 %collective-permute-done.35 = bf16[96,768]{1,0:T(8,128)(2,1)S(1)} collective-permute-done((bf16[96,768]{1,0:T(8,128)(2,1)S(1)}, bf16[96,768]{1,0:T(8,128)(2,1)S(1)}, u32[]{:S(2)}, u32[]{:S(2)}) %collective-permute-start.35) | collective-permute-done | bytes 147488 | tf_op jit(solution)/shard_map/ppermute | solution.py:20
  (494 shorter events, 312.1 us)
Async XLA Ops:
  4.2 15.5 %collective-permute-start.8 = (bf16[1536]{0:T(1024)(128)(2,1)S(1)}, bf16[1536]{0:T(1024)(128)(2,1)S(1)}, u32[]{:S(2)}, u32[]{:S(2)}) collective-permute-start(bf16[1536]{0:T(1024)(128)(2,1)S(1)} %concatenate.99), channel_id=1, source_target_pairs={{0,2},{1,3},{2,0},{3,1},{4,6},{5,7},{6,4},{7,5},{8,10},{9,11},{10,... | collective-permute-start | bytes 9224 | tf_op jit(solution)/shard_map/ppermute | solution.py:20
  14.3 22.9 %collective-permute-start = (bf16[96,768]{1,0:T(8,128)(2,1)S(1)}, bf16[96,768]{1,0:T(8,128)(2,1)S(1)}, u32[]{:S(2)}, u32[]{:S(2)}) collective-permute-start(bf16[96,768]{1,0:T(8,128)(2,1)S(1)} %pad_maximum_fusion.34), channel_id=1, source_target_pairs={{0,2},{1,3},{2,0},{3,1},{4,6},{5,7},{6,4},{7,5},{8,10},{9,11},{10,... | collective-permute-start | bytes 442376 | tf_op jit(solution)/shard_map/ppermute | solution.py:20
  14.7 22.5 %collective-permute-start.10 = (bf16[96,768]{1,0:T(8,128)(2,1)}, bf16[96,768]{1,0:T(8,128)(2,1)S(1)}, u32[]{:S(2)}, u32[]{:S(2)}) collective-permute-start(bf16[96,768]{1,0:T(8,128)(2,1)} %param.23), channel_id=1, source_target_pairs={{0,2},{1,3},{2,0},{3,1},{4,6},{5,7},{6,4},{7,5},{8,10},{9,11},{10,... | collective-permute-start | bytes 442376 | tf_op jit(solution)/shard_map/ppermute | solution.py:20
  17.3 23.2 %collective-permute-start.18 = (bf16[384,192]{0,1:T(8,128)(2,1)}, bf16[384,192]{0,1:T(8,128)(2,1)S(1)}, u32[]{:S(2)}, u32[]{:S(2)}) collective-permute-start(bf16[384,192]{0,1:T(8,128)(2,1)} %param.25), channel_id=1, source_target_pairs={{0,2},{1,3},{2,0},{3,1},{4,6},{5,7},{6,4},{7,5},{8,10},{9,11},{10,... | collective-permute-start | bytes 442376 | tf_op jit(solution)/shard_map/ppermute | solution.py:20
  40.6 16.4 %collective-permute-start.19 = (bf16[2,384,192]{1,2,0:T(8,128)(2,1)S(1)}, bf16[2,384,192]{1,2,0:T(8,128)(2,1)S(1)}, u32[]{:S(2)}, u32[]{:S(2)}) collective-permute-start(bf16[2,384,192]{1,2,0:T(8,128)(2,1)S(1)} %pad_maximum_fusion.33), channel_id=1, source_target_pairs={{0,1},{1,0},{2,3},{3,2},{4,5},{5,4},{6,7},{7,6},{8,9},{9,8},{10,11... | collective-permute-start | bytes 884744 | tf_op jit(solution)/shard_map/ppermute | solution.py:20
  41.4 22.9 %collective-permute-start.11 = (bf16[2,96,768]{2,1,0:T(8,128)(2,1)}, bf16[2,96,768]{2,1,0:T(8,128)(2,1)}, u32[]{:S(2)}, u32[]{:S(2)}) collective-permute-start(bf16[2,96,768]{2,1,0:T(8,128)(2,1)} %pad_maximum_fusion.32), channel_id=1, source_target_pairs={{0,1},{1,0},{2,3},{3,2},{4,5},{5,4},{6,7},{7,6},{8,9},{9,8},{10,11... | collective-permute-start | bytes 884744 | tf_op jit(solution)/shard_map/ppermute | solution.py:20
  43.4 31.7 %all-to-all-start = ((bf16[4,64,768]{2,1,0:T(8,128)(2,1)}), bf16[4,64,768]{2,1,0:T(8,128)(2,1)S(1)}, u32[]{:S(2)}, u32[]{:S(2)}) async-start(bf16[4,64,768]{2,1,0:T(8,128)(2,1)} %bitcast), calls=%async_computation | async-start | bytes 786432 | tf_op jit(solution)/shard_map/all_to_all | solution.py:180
  69.3 47.2 %collective-permute-start.23 = (bf16[4,96,384]{1,2,0:T(8,128)(2,1)}, bf16[4,96,384]{1,2,0:T(8,128)(2,1)}, u32[]{:S(2)}, u32[]{:S(2)}) collective-permute-start(bf16[4,96,384]{1,2,0:T(8,128)(2,1)} %copy.348), channel_id=1, source_target_pairs={{0,16},{4,20},{8,24},{12,28},{16,0},{20,4},{24,8},{28,12},{1,17},{... | collective-permute-start | bytes 884744 | tf_op jit(solution)/shard_map/ppermute | solution.py:20
  69.9 57.8 %collective-permute-start.20 = (bf16[4,96,384]{1,2,0:T(8,128)(2,1)}, bf16[4,96,384]{1,2,0:T(8,128)(2,1)}, u32[]{:S(2)}, u32[]{:S(2)}) collective-permute-start(bf16[4,96,384]{1,2,0:T(8,128)(2,1)} %copy.347), channel_id=1, source_target_pairs={{0,8},{4,12},{8,0},{12,4},{16,24},{20,28},{24,16},{28,20},{1,9},{5... | collective-permute-start | bytes 884744 | tf_op jit(solution)/shard_map/ppermute | solution.py:20
  70.6 40.5 %collective-permute-start.15 = (bf16[4,96,384]{1,2,0:T(8,128)(2,1)}, bf16[4,96,384]{1,2,0:T(8,128)(2,1)}, u32[]{:S(2)}, u32[]{:S(2)}) collective-permute-start(bf16[4,96,384]{1,2,0:T(8,128)(2,1)} %copy.346), channel_id=1, source_target_pairs={{0,16},{4,20},{8,24},{12,28},{16,0},{20,4},{24,8},{28,12},{1,17},{... | collective-permute-start | bytes 884744 | tf_op jit(solution)/shard_map/ppermute | solution.py:20
  72.1 50.2 %collective-permute-start.12 = (bf16[4,96,384]{1,2,0:T(8,128)(2,1)}, bf16[4,96,384]{1,2,0:T(8,128)(2,1)}, u32[]{:S(2)}, u32[]{:S(2)}) collective-permute-start(bf16[4,96,384]{1,2,0:T(8,128)(2,1)} %copy.345), channel_id=1, source_target_pairs={{0,8},{4,12},{8,0},{12,4},{16,24},{20,28},{24,16},{28,20},{1,9},{5... | collective-permute-start | bytes 884744 | tf_op jit(solution)/shard_map/ppermute | solution.py:20
  74.4 19.6 %collective-permute-start.2 = (bf16[4,96,384]{1,2,0:T(8,128)(2,1)}, bf16[4,96,384]{1,2,0:T(8,128)(2,1)S(1)}, u32[]{:S(2)}, u32[]{:S(2)}) collective-permute-start(bf16[4,96,384]{1,2,0:T(8,128)(2,1)} %get-tuple-element.97), channel_id=1, source_target_pairs={{0,8},{4,12},{8,0},{12,4},{16,24},{20,28},{24,16},{28,20},{1,9},{5... | collective-permute-start | bytes 884744 | tf_op jit(solution)/shard_map/ppermute | solution.py:20
  75.1 13.4 %all-to-all-start.5 = ((bf16[4,64,768]{2,1,0:T(8,128)(2,1)}), bf16[4,64,768]{2,1,0:T(8,128)(2,1)S(1)}, u32[]{:S(2)}, u32[]{:S(2)}) async-start(bf16[4,64,768]{2,1,0:T(8,128)(2,1)} %bitcast.100), calls=%async_computation.5 | async-start | bytes 786432 | tf_op jit(solution)/shard_map/all_to_all | solution.py:180
  105.1 79.1 %collective-permute-start.3 = (bf16[2,4,96,384]{3,2,1,0:T(8,128)(2,1)}, bf16[2,4,96,384]{3,2,1,0:T(8,128)(2,1)}, u32[]{:S(2)}, u32[]{:S(2)}) collective-permute-start(bf16[2,4,96,384]{3,2,1,0:T(8,128)(2,1)} %copy.250), channel_id=1, source_target_pairs={{0,16},{4,20},{8,24},{12,28},{16,0},{20,4},{24,8},{28,12},{1,17},{... | collective-permute-start | bytes 1769480 | tf_op jit(solution)/shard_map/ppermute | solution.py:20
  111.1 55.0 %collective-permute-start.6 = (bf16[2,4,96,384]{3,2,1,0:T(8,128)(2,1)}, bf16[2,4,96,384]{3,2,1,0:T(8,128)(2,1)}, u32[]{:S(2)}, u32[]{:S(2)}) collective-permute-start(bf16[2,4,96,384]{3,2,1,0:T(8,128)(2,1)} %copy.257), channel_id=1, source_target_pairs={{0,8},{4,12},{8,0},{12,4},{16,24},{20,28},{24,16},{28,20},{1,9},{5... | collective-permute-start | bytes 1769480 | tf_op jit(solution)/shard_map/ppermute | solution.py:20
  116.5 20.1 %collective-permute-start.16 = (bf16[2,4,96,384]{3,2,1,0:T(8,128)(2,1)}, bf16[2,4,96,384]{3,2,1,0:T(8,128)(2,1)}, u32[]{:S(2)}, u32[]{:S(2)}) collective-permute-start(bf16[2,4,96,384]{3,2,1,0:T(8,128)(2,1)} %copy.280), channel_id=1, source_target_pairs={{0,8},{4,12},{8,0},{12,4},{16,24},{20,28},{24,16},{28,20},{1,9},{5... | collective-permute-start | bytes 1769480 | tf_op jit(solution)/shard_map/ppermute | solution.py:20
  122.3 20.6 %collective-permute-start.24 = (bf16[2,4,96,384]{3,2,1,0:T(8,128)(2,1)}, bf16[2,4,96,384]{3,2,1,0:T(8,128)(2,1)}, u32[]{:S(2)}, u32[]{:S(2)}) collective-permute-start(bf16[2,4,96,384]{3,2,1,0:T(8,128)(2,1)} %copy.299), channel_id=1, source_target_pairs={{0,8},{4,12},{8,0},{12,4},{16,24},{20,28},{24,16},{28,20},{1,9},{5... | collective-permute-start | bytes 1769480 | tf_op jit(solution)/shard_map/ppermute | solution.py:20
  127.6 47.3 %collective-permute-start.13 = (bf16[2,4,96,384]{3,2,1,0:T(8,128)(2,1)}, bf16[2,4,96,384]{3,2,1,0:T(8,128)(2,1)}, u32[]{:S(2)}, u32[]{:S(2)}) collective-permute-start(bf16[2,4,96,384]{3,2,1,0:T(8,128)(2,1)} %copy.272), channel_id=1, source_target_pairs={{0,16},{4,20},{8,24},{12,28},{16,0},{20,4},{24,8},{28,12},{1,17},{... | collective-permute-start | bytes 1769480 | tf_op jit(solution)/shard_map/ppermute | solution.py:20
  136.6 16.3 %collective-permute-start.21 = (bf16[2,4,96,384]{3,2,1,0:T(8,128)(2,1)}, bf16[2,4,96,384]{3,2,1,0:T(8,128)(2,1)}, u32[]{:S(2)}, u32[]{:S(2)}) collective-permute-start(bf16[2,4,96,384]{3,2,1,0:T(8,128)(2,1)} %copy.291), channel_id=1, source_target_pairs={{0,16},{4,20},{8,24},{12,28},{16,0},{20,4},{24,8},{28,12},{1,17},{... | collective-permute-start | bytes 1769480 | tf_op jit(solution)/shard_map/ppermute | solution.py:20
  152.8 40.2 %collective-permute-start.25 = (bf16[2,2,4,96,384]{4,3,2,1,0:T(8,128)(2,1)}, bf16[2,2,4,96,384]{4,3,2,1,0:T(8,128)(2,1)}, u32[]{:S(2)}, u32[]{:S(2)}) collective-permute-start(bf16[2,2,4,96,384]{4,3,2,1,0:T(8,128)(2,1)} %copy.302), channel_id=1, source_target_pairs={{0,4},{4,0},{8,12},{12,8},{16,20},{20,16},{24,28},{28,24},{1,5},{5... | collective-permute-start | bytes 3538952 | tf_op jit(solution)/shard_map/ppermute | solution.py:20
  161.6 34.5 %collective-permute-start.22 = (bf16[2,2,4,96,384]{4,3,2,1,0:T(8,128)(2,1)}, bf16[2,2,4,96,384]{4,3,2,1,0:T(8,128)(2,1)}, u32[]{:S(2)}, u32[]{:S(2)}) collective-permute-start(bf16[2,2,4,96,384]{4,3,2,1,0:T(8,128)(2,1)} %copy.294), channel_id=1, source_target_pairs={{0,4},{4,0},{8,12},{12,8},{16,20},{20,16},{24,28},{28,24},{1,5},{5... | collective-permute-start | bytes 3538952 | tf_op jit(solution)/shard_map/ppermute | solution.py:20
  166.1 32.5 %collective-permute-start.17 = (bf16[2,2,4,96,384]{4,3,2,1,0:T(8,128)(2,1)}, bf16[2,2,4,96,384]{4,3,2,1,0:T(8,128)(2,1)}, u32[]{:S(2)}, u32[]{:S(2)}) collective-permute-start(bf16[2,2,4,96,384]{4,3,2,1,0:T(8,128)(2,1)} %copy.283), channel_id=1, source_target_pairs={{0,4},{4,0},{8,12},{12,8},{16,20},{20,16},{24,28},{28,24},{1,5},{5... | collective-permute-start | bytes 3538952 | tf_op jit(solution)/shard_map/ppermute | solution.py:20
  174.9 31.1 %collective-permute-start.7 = (bf16[2,2,4,96,384]{4,3,2,1,0:T(8,128)(2,1)}, bf16[2,2,4,96,384]{4,3,2,1,0:T(8,128)(2,1)}, u32[]{:S(2)}, u32[]{:S(2)}) collective-permute-start(bf16[2,2,4,96,384]{4,3,2,1,0:T(8,128)(2,1)} %copy.260), channel_id=1, source_target_pairs={{0,4},{4,0},{8,12},{12,8},{16,20},{20,16},{24,28},{28,24},{1,5},{5... | collective-permute-start | bytes 3538952 | tf_op jit(solution)/shard_map/ppermute | solution.py:20
  184.2 67.0 %collective-permute-start.14 = (bf16[2,2,4,96,384]{4,3,2,1,0:T(8,128)(2,1)}, bf16[2,2,4,96,384]{4,3,2,1,0:T(8,128)(2,1)}, u32[]{:S(2)}, u32[]{:S(2)}) collective-permute-start(bf16[2,2,4,96,384]{4,3,2,1,0:T(8,128)(2,1)} %copy.275), channel_id=1, source_target_pairs={{0,4},{4,0},{8,12},{12,8},{16,20},{20,16},{24,28},{28,24},{1,5},{5... | collective-permute-start | bytes 3538952 | tf_op jit(solution)/shard_map/ppermute | solution.py:20
  193.1 42.0 %collective-permute-start.4 = (bf16[2,2,4,96,384]{4,3,2,1,0:T(8,128)(2,1)}, bf16[2,2,4,96,384]{4,3,2,1,0:T(8,128)(2,1)}, u32[]{:S(2)}, u32[]{:S(2)}) collective-permute-start(bf16[2,2,4,96,384]{4,3,2,1,0:T(8,128)(2,1)} %copy.253), channel_id=1, source_target_pairs={{0,4},{4,0},{8,12},{12,8},{16,20},{20,16},{24,28},{28,24},{1,5},{5... | collective-permute-start | bytes 3538952 | tf_op jit(solution)/shard_map/ppermute | solution.py:20
  351.5 116.1 %collective-permute-start.44 = (bf16[2,2,4,96,384]{4,3,2,1,0:T(8,128)(2,1)}, bf16[2,2,4,96,384]{4,3,2,1,0:T(8,128)(2,1)}, u32[]{:S(2)}, u32[]{:S(2)}) collective-permute-start(bf16[2,2,4,96,384]{4,3,2,1,0:T(8,128)(2,1)} %dynamic-slice_bitcast_fusion), channel_id=1, source_target_pairs={{0,4},{4,0},{8,12},{12,8},{16,20},{20,16},{24,28},{28,24},{1,5},{5... | collective-permute-start | bytes 3538952 | tf_op jit(solution)/shard_map/ppermute | solution.py:20
  351.5 118.6 %collective-permute-start.47 = (bf16[2,2,4,96,384]{4,3,2,1,0:T(8,128)(2,1)}, bf16[2,2,4,96,384]{4,3,2,1,0:T(8,128)(2,1)}, u32[]{:S(2)}, u32[]{:S(2)}) collective-permute-start(bf16[2,2,4,96,384]{4,3,2,1,0:T(8,128)(2,1)} %bitcast.431), channel_id=1, source_target_pairs={{0,4},{4,0},{8,12},{12,8},{16,20},{20,16},{24,28},{28,24},{1,5},{5... | collective-permute-start | bytes 3538952 | tf_op jit(solution)/shard_map/ppermute | solution.py:20
  384.7 88.9 %collective-permute-start.36 = (bf16[2,2,4,96,384]{4,3,2,1,0:T(8,128)(2,1)}, bf16[2,2,4,96,384]{4,3,2,1,0:T(8,128)(2,1)}, u32[]{:S(2)}, u32[]{:S(2)}) collective-permute-start(bf16[2,2,4,96,384]{4,3,2,1,0:T(8,128)(2,1)} %dynamic-slice_bitcast_fusion.1), channel_id=1, source_target_pairs={{0,4},{4,0},{8,12},{12,8},{16,20},{20,16},{24,28},{28,24},{1,5},{5... | collective-permute-start | bytes 3538952 | tf_op jit(solution)/shard_map/ppermute | solution.py:20
  384.7 92.2 %collective-permute-start.39 = (bf16[2,2,4,96,384]{4,3,2,1,0:T(8,128)(2,1)}, bf16[2,2,4,96,384]{4,3,2,1,0:T(8,128)(2,1)}, u32[]{:S(2)}, u32[]{:S(2)}) collective-permute-start(bf16[2,2,4,96,384]{4,3,2,1,0:T(8,128)(2,1)} %bitcast.432), channel_id=1, source_target_pairs={{0,4},{4,0},{8,12},{12,8},{16,20},{20,16},{24,28},{28,24},{1,5},{5... | collective-permute-start | bytes 3538952 | tf_op jit(solution)/shard_map/ppermute | solution.py:20
  394.9 24.0 %all-to-all-start.8 = ((f32[8,4,96]{2,1,0:T(4,128)}), f32[8,4,96]{2,1,0:T(4,128)S(1)}, u32[]{:S(2)}, u32[]{:S(2)}) async-start(f32[8,4,96]{2,1,0:T(4,128)} %bitcast.116), calls=%async_computation.8 | async-start | bytes 32768 | tf_op jit(solution)/shard_map/all_to_all | solution.py:280
  418.8 23.9 %all-to-all-start.4 = ((bf16[4,2,24576]{2,1,0:T(2,128)(2,1)}), bf16[4,2,24576]{2,1,0:T(2,128)(2,1)}, u32[]{:S(2)}, u32[]{:S(2)}) async-start(bf16[4,2,24576]{2,1,0:T(2,128)(2,1)} %reshape.1001), calls=%async_computation.4 | async-start | bytes 786432 | tf_op jit(solution)/shard_map/all_to_all | solution.py:183
  442.8 21.9 %all-to-all-start.6 = ((bf16[4,2,24576]{2,1,0:T(2,128)(2,1)}), bf16[4,2,24576]{2,1,0:T(2,128)(2,1)}, u32[]{:S(2)}, u32[]{:S(2)}) async-start(bf16[4,2,24576]{2,1,0:T(2,128)(2,1)} %reshape.1003), calls=%async_computation.6 | async-start | bytes 786432 | tf_op jit(solution)/shard_map/all_to_all | solution.py:183
  461.1 18.1 %collective-permute-start.31 = (bf16[2,2,4,96,384]{4,3,2,1,0:T(8,128)(2,1)}, bf16[2,2,4,96,384]{4,3,2,1,0:T(8,128)(2,1)}, u32[]{:S(2)}, u32[]{:S(2)}) collective-permute-start(bf16[2,2,4,96,384]{4,3,2,1,0:T(8,128)(2,1)} %bitcast.496), channel_id=1, source_target_pairs={{0,4},{4,0},{8,12},{12,8},{16,20},{20,16},{24,28},{28,24},{1,5},{5... | collective-permute-start | bytes 3538952 | tf_op jit(solution)/shard_map/ppermute | solution.py:20
  467.6 13.9 %collective-permute-start.28 = (bf16[2,2,4,96,384]{4,3,2,1,0:T(8,128)(2,1)}, bf16[2,2,4,96,384]{4,3,2,1,0:T(8,128)(2,1)S(1)}, u32[]{:S(2)}, u32[]{:S(2)}) collective-permute-start(bf16[2,2,4,96,384]{4,3,2,1,0:T(8,128)(2,1)} %dynamic-slice_bitcast_fusion.2), channel_id=1, source_target_pairs={{0,4},{4,0},{8,12},{12,8},{16,20},{20,16},{24,28},{28,24},{1,5},{5... | collective-permute-start | bytes 3538952 | tf_op jit(solution)/shard_map/ppermute | solution.py:20
  470.1 16.2 %collective-permute-start.45 = (bf16[2,4,96,384]{3,2,1,0:T(8,128)(2,1)S(1)}, bf16[2,4,96,384]{3,2,1,0:T(8,128)(2,1)S(1)}, u32[]{:S(2)}, u32[]{:S(2)}) collective-permute-start(bf16[2,4,96,384]{3,2,1,0:T(8,128)(2,1)S(1)} %fusion.49), channel_id=1, source_target_pairs={{0,16},{4,20},{8,24},{12,28},{16,0},{20,4},{24,8},{28,12},{1,17},{... | collective-permute-start | bytes 1769480 | tf_op jit(solution)/shard_map/ppermute | solution.py:20
  473.6 16.3 %collective-permute-start.48 = (bf16[2,4,96,384]{3,2,1,0:T(8,128)(2,1)S(1)}, bf16[2,4,96,384]{3,2,1,0:T(8,128)(2,1)S(1)}, u32[]{:S(2)}, u32[]{:S(2)}) collective-permute-start(bf16[2,4,96,384]{3,2,1,0:T(8,128)(2,1)S(1)} %fusion.50), channel_id=1, source_target_pairs={{0,8},{4,12},{8,0},{12,4},{16,24},{20,28},{24,16},{28,20},{1,9},{5... | collective-permute-start | bytes 1769480 | tf_op jit(solution)/shard_map/ppermute | solution.py:20
  476.8 22.2 %collective-permute-start.37 = (bf16[2,4,96,384]{3,2,1,0:T(8,128)(2,1)S(1)}, bf16[2,4,96,384]{3,2,1,0:T(8,128)(2,1)S(1)}, u32[]{:S(2)}, u32[]{:S(2)}) collective-permute-start(bf16[2,4,96,384]{3,2,1,0:T(8,128)(2,1)S(1)} %fusion.47), channel_id=1, source_target_pairs={{0,16},{4,20},{8,24},{12,28},{16,0},{20,4},{24,8},{28,12},{1,17},{... | collective-permute-start | bytes 1769480 | tf_op jit(solution)/shard_map/ppermute | solution.py:20
  479.2 23.3 %collective-permute-start.40 = (bf16[2,4,96,384]{3,2,1,0:T(8,128)(2,1)S(1)}, bf16[2,4,96,384]{3,2,1,0:T(8,128)(2,1)S(1)}, u32[]{:S(2)}, u32[]{:S(2)}) collective-permute-start(bf16[2,4,96,384]{3,2,1,0:T(8,128)(2,1)S(1)} %fusion.48), channel_id=1, source_target_pairs={{0,8},{4,12},{8,0},{12,4},{16,24},{20,28},{24,16},{28,20},{1,9},{5... | collective-permute-start | bytes 1769480 | tf_op jit(solution)/shard_map/ppermute | solution.py:20
  481.5 33.7 %collective-permute-start.32 = (bf16[2,4,96,384]{3,2,1,0:T(8,128)(2,1)S(1)}, bf16[2,4,96,384]{3,2,1,0:T(8,128)(2,1)S(1)}, u32[]{:S(2)}, u32[]{:S(2)}) collective-permute-start(bf16[2,4,96,384]{3,2,1,0:T(8,128)(2,1)S(1)} %fusion.46), channel_id=1, source_target_pairs={{0,8},{4,12},{8,0},{12,4},{16,24},{20,28},{24,16},{28,20},{1,9},{5... | collective-permute-start | bytes 1769480 | tf_op jit(solution)/shard_map/ppermute | solution.py:20
  486.4 30.1 %collective-permute-start.29 = (bf16[2,4,96,384]{3,2,1,0:T(8,128)(2,1)S(1)}, bf16[2,4,96,384]{3,2,1,0:T(8,128)(2,1)S(1)}, u32[]{:S(2)}, u32[]{:S(2)}) collective-permute-start(bf16[2,4,96,384]{3,2,1,0:T(8,128)(2,1)S(1)} %fusion.45), channel_id=1, source_target_pairs={{0,16},{4,20},{8,24},{12,28},{16,0},{20,4},{24,8},{28,12},{1,17},{... | collective-permute-start | bytes 1769480 | tf_op jit(solution)/shard_map/ppermute | solution.py:20
  489.9 31.6 %collective-permute-start.46 = (bf16[4,96,384]{2,1,0:T(8,128)(2,1)S(1)}, bf16[4,96,384]{2,1,0:T(8,128)(2,1)S(1)}, u32[]{:S(2)}, u32[]{:S(2)}) collective-permute-start(bf16[4,96,384]{2,1,0:T(8,128)(2,1)S(1)} %fusion.61), channel_id=1, source_target_pairs={{0,8},{4,12},{8,0},{12,4},{16,24},{20,28},{24,16},{28,20},{1,9},{5... | collective-permute-start | bytes 884744 | tf_op jit(solution)/shard_map/ppermute | solution.py:20
  499.0 24.0 %collective-permute-start.49 = (bf16[4,96,384]{2,1,0:T(8,128)(2,1)S(1)}, bf16[4,96,384]{2,1,0:T(8,128)(2,1)S(1)}, u32[]{:S(2)}, u32[]{:S(2)}) collective-permute-start(bf16[4,96,384]{2,1,0:T(8,128)(2,1)S(1)} %fusion.62), channel_id=1, source_target_pairs={{0,16},{4,20},{8,24},{12,28},{16,0},{20,4},{24,8},{28,12},{1,17},{... | collective-permute-start | bytes 884744 | tf_op jit(solution)/shard_map/ppermute | solution.py:20
  502.5 26.2 %collective-permute-start.38 = (bf16[4,96,384]{2,1,0:T(8,128)(2,1)S(1)}, bf16[4,96,384]{2,1,0:T(8,128)(2,1)}, u32[]{:S(2)}, u32[]{:S(2)}) collective-permute-start(bf16[4,96,384]{2,1,0:T(8,128)(2,1)S(1)} %fusion.58), channel_id=1, source_target_pairs={{0,8},{4,12},{8,0},{12,4},{16,24},{20,28},{24,16},{28,20},{1,9},{5... | collective-permute-start | bytes 884744 | tf_op jit(solution)/shard_map/ppermute | solution.py:20
  515.2 14.6 %collective-permute-start.41 = (bf16[4,96,384]{2,1,0:T(8,128)(2,1)}, bf16[4,96,384]{2,1,0:T(8,128)(2,1)}, u32[]{:S(2)}, u32[]{:S(2)}) collective-permute-start(bf16[4,96,384]{2,1,0:T(8,128)(2,1)} %fusion.59), channel_id=1, source_target_pairs={{0,16},{4,20},{8,24},{12,28},{16,0},{20,4},{24,8},{28,12},{1,17},{... | collective-permute-start | bytes 884744 | tf_op jit(solution)/shard_map/ppermute | solution.py:20
  516.4 16.6 %collective-permute-start.33 = (bf16[4,96,384]{2,1,0:T(8,128)(2,1)}, bf16[4,96,384]{2,1,0:T(8,128)(2,1)}, u32[]{:S(2)}, u32[]{:S(2)}) collective-permute-start(bf16[4,96,384]{2,1,0:T(8,128)(2,1)} %fusion.56), channel_id=1, source_target_pairs={{0,16},{4,20},{8,24},{12,28},{16,0},{20,4},{24,8},{28,12},{1,17},{... | collective-permute-start | bytes 884744 | tf_op jit(solution)/shard_map/ppermute | solution.py:20
  521.5 12.6 %collective-permute-start.30 = (bf16[4,96,384]{2,1,0:T(8,128)(2,1)}, bf16[4,96,384]{2,1,0:T(8,128)(2,1)}, u32[]{:S(2)}, u32[]{:S(2)}) collective-permute-start(bf16[4,96,384]{2,1,0:T(8,128)(2,1)} %fusion.55), channel_id=1, source_target_pairs={{0,8},{4,12},{8,0},{12,4},{16,24},{20,28},{24,16},{28,20},{1,9},{5... | collective-permute-start | bytes 884744 | tf_op jit(solution)/shard_map/ppermute | solution.py:20
  531.7 20.3 %collective-permute-start.42 = (bf16[2,96,768]{2,1,0:T(8,128)(2,1)}, bf16[2,96,768]{2,1,0:T(8,128)(2,1)}, u32[]{:S(2)}, u32[]{:S(2)}) collective-permute-start(bf16[2,96,768]{2,1,0:T(8,128)(2,1)} %fusion.60), channel_id=1, source_target_pairs={{0,1},{1,0},{2,3},{3,2},{4,5},{5,4},{6,7},{7,6},{8,9},{9,8},{10,11... | collective-permute-start | bytes 884744 | tf_op jit(solution)/shard_map/ppermute | solution.py:20
  540.5 23.8 %collective-permute-start.51 = (bf16[384,192]{0,1:T(8,128)(2,1)S(1)}, bf16[384,192]{0,1:T(8,128)(2,1)S(1)}, u32[]{:S(2)}, u32[]{:S(2)}) collective-permute-start(bf16[384,192]{0,1:T(8,128)(2,1)S(1)} %fusion.76), channel_id=1, source_target_pairs={{0,2},{1,3},{2,0},{3,1},{4,6},{5,7},{6,4},{7,5},{8,10},{9,11},{10,... | collective-permute-start | bytes 442376 | tf_op jit(solution)/shard_map/ppermute | solution.py:20
  (83 other events, 529.4 us)
